TPU v7x, 128 devices: a whole 4x4x4 slice. The times are simulated.
128 devices in a mesh: row: 8 (over y, core), grp: 16 (over x, z).
Axes of the slice: x: 4, y: 4, z: 4, core: 2. Of those that a mesh axis runs over, the one named last changes fastest.
Arguments:
- embeddings: bfloat16 [57344, 1024], P(('row', 'grp')), may hold values from -16 to 16
- scales: float32 [57344, 8], P(('row', 'grp')), may hold values from 0.3 to 3
- cluster_id: int32 [57344], P(('row', 'grp')), may hold values from 0 to 7, as said below
- doc_rank: int32 [57344], P(('row', 'grp')), may hold values from 0 to 14335, as said below
Outputs:
- nearest: float32 [57344], P(('row', 'grp'))
Inputs may be any that keep to these rules, and one draw needn't show every extreme that they name: `cluster_id`: within each cluster the doc_rank values are 0, 1, and so on up to the cluster's size less one, each once; some cluster has exactly 14336 documents. `doc_rank`: counting a document of cluster c and rank k toward slot group c * 16 + (k mod 16), each aligned block of 448 documents holds at most 7 documents of any one slot group, and in every draw some slot group has exactly 7 documents in every block.
All inputs are finite; a program needn't handle non-finite values.
Results may differ from a plain program's by a relative error of at most 0.00068.
Values may be sent and summed in bfloat16 or wider, within the bound.
A program may use at most 128 MiB of HBM per device.

v0:
```python
import jax
import jax.numpy as jnp
from jax import lax
from jax.sharding import PartitionSpec as P


def unit_rows(embeddings, scales):
    doc_count, feature_dim = embeddings.shape
    blocks = scales.shape[1]
    scaled = (
        embeddings.astype(jnp.float32).reshape(doc_count, blocks, feature_dim // blocks)
        * scales[:, :, None]
    ).reshape(doc_count, feature_dim)
    squares = jnp.sum(scaled * scaled, axis=1, keepdims=True)
    return (scaled * lax.rsqrt(squares + 1e-06)).astype(jnp.bfloat16)


def local(embeddings, scales, cluster_id, doc_rank):
    group_size = lax.axis_size("grp")
    row_count = lax.axis_size("row")
    devices = group_size * row_count
    doc_count, feature_dim = embeddings.shape
    slot_count = 2 * doc_count
    per_peer = slot_count // devices
    unit_vecs = unit_rows(embeddings, scales)
    target = cluster_id * group_size + doc_rank % group_size
    onehot = (target[:, None] == jnp.arange(devices, dtype=jnp.int32)[None, :]).astype(jnp.int32)
    before = jnp.sum(jnp.cumsum(onehot, axis=0) * onehot, axis=1) - 1
    position = target * per_peer + before
    outgoing = jnp.zeros((slot_count, feature_dim), jnp.bfloat16).at[position].set(unit_vecs)
    labels = jnp.zeros((slot_count,), jnp.int32).at[position].set(doc_rank // group_size + 1)
    arrived, slot_tags = (
        lax.all_to_all(outgoing, ("row", "grp"), split_axis=0, concat_axis=0, tiled=True),
        lax.all_to_all(labels, ("row", "grp"), split_axis=0, concat_axis=0, tiled=True),
    )
    slot_index = jnp.where(slot_tags > 0, slot_tags - 1, slot_count)
    members = (
        jnp.zeros((slot_count, feature_dim), jnp.bfloat16).at[slot_index].set(arrived, mode="drop")
    )
    own_place = lax.axis_index("grp")
    own_rank = jnp.arange(slot_count, dtype=jnp.int32) * group_size + own_place
    floor_value = jnp.full((slot_count,), -1.0, jnp.float32)
    piece = lax.all_gather(members, "grp", axis=0, tiled=True)
    indices = jnp.arange(piece.shape[0], dtype=jnp.int32)
    piece_rank = indices % slot_count * group_size + indices // slot_count
    scores = lax.dot_general(
        members, piece, (((1,), (1,)), ((), ())), preferred_element_type=jnp.float32
    )
    masked = jnp.where(piece_rank[None, :] < own_rank[:, None], scores, -1.0)
    best_sim = jnp.maximum(floor_value, jnp.max(masked, axis=1))
    replies = best_sim[jnp.minimum(slot_index, slot_count - 1)]
    answers = lax.all_to_all(replies, ("row", "grp"), split_axis=0, concat_axis=0, tiled=True)
    return answers[position]


def solution(mesh):
    return jax.shard_map(
        local,
        mesh=mesh,
        in_specs=(
            P(("row", "grp"), None),
            P(("row", "grp"), None),
            P(("row", "grp")),
            P(("row", "grp")),
        ),
        out_specs=P(("row", "grp")),
        check_vma=False,
    )
```

profile of v0, /device:TPU:1, one launch (start us, length us, event | category | flops | bytes accessed | tf_op | source)
XLA Modules:
  0.0 317.9 jit_solution(8619993745614739836)
XLA Ops:
  6.5 0.7 fusion.21
  7.3 0.1 iota_compare_fusion
  7.4 0.2 fusion.5
  7.7 0.2 fusion.7
  8.0 2.9 scatter_custom_fusion
  10.9 0.8 all_to_all.22
  11.7 11.5 %all-to-all-start = ((s32[128,7,1]{1,2,0:T(1,128)}), s32[128,7,1]{1,2,0:T(1,128)S(1)}, u32[]{:S(2)}, u32[]{:S(2)}) async-start(s32[128,7,1]{1,2,0:T(1,128)} %bitcast.4), calls=%async_computation | async-start | bytes 131072 | tf_op jit(solution)/shard_map/all_to_all | solution.py:34
  23.2 0.0 copy-done.2
  23.2 0.1 copy.12
  23.4 0.5 mul.66
  23.9 0.4 multiply_reduce_fusion
  24.3 4.0 %scatter_custom_fusion.1 = bf16[896,1024]{1,0:T(8,128)(2,1)} fusion(s32[448]{0:T(512)S(1)} %compare_select_fusion.3, f32[56,8,8,128]{3,2,1,0:T(8,128)S(1)} %bitcast.23, bf16[448,1024]{1,0:T(8,128)(2,1)S(1)} %copy-done.1, f32[448]{0:T(512)S(1)} %add_rsqrt_fusion, bf16[]{:T(256)} %constant.72.clone.1), kind=kCustom, calls=%fused_computation.9 | custom fusion | flops 1835008 | bytes 4589570 | tf_op jit(solution)/shard_map/scatter | solution.py:30
  28.3 3.9 %all_to_all.24 = bf16[128,7,1024]{2,1,0:T(8,128)(2,1)} reshape(bf16[896,1024]{1,0:T(8,128)(2,1)} %scatter_custom_fusion.1) | data formatting | bytes 3670016 | tf_op jit(solution)/shard_map/all_to_all | solution.py:33
  32.2 0.5 all-to-all-done
  32.7 9.2 %all-to-all-start.1 = ((bf16[128,7,1024]{2,1,0:T(8,128)(2,1)}), bf16[128,7,1024]{2,1,0:T(8,128)(2,1)S(1)}, u32[]{:S(2)}, u32[]{:S(2)}) async-start(bf16[128,7,1024]{2,1,0:T(8,128)(2,1)} %all_to_all.24), calls=%async_computation.1 | async-start | bytes 4194304 | tf_op jit(solution)/shard_map/all_to_all | solution.py:33
  42.0 0.0 all-gather.2.cloned.1.call-start
  42.0 0.2 fusion.12
  42.2 0.2 select_n.84
  42.5 29.1 %all-to-all-done.1 = bf16[128,7,1024]{2,1,0:T(8,128)(2,1)S(1)} async-done(((bf16[128,7,1024]{2,1,0:T(8,128)(2,1)}), bf16[128,7,1024]{2,1,0:T(8,128)(2,1)S(1)}, u32[]{:S(2)}, u32[]{:S(2)}) %all-to-all-start.1) | async-done | bytes 1835040 | tf_op jit(solution)/shard_map/all_to_all | solution.py:33
  71.6 1.6 reshape.147
  73.2 7.8 %scatter_custom_fusion.2 = bf16[896,1024]{1,0:T(8,128)(2,1)} fusion(s32[896]{0:T(1024)S(1)} %get-tuple-element.6, bf16[896,1024]{1,0:T(8,128)(2,1)} %reshape.147, bf16[]{:T(256)} %constant.72.clone.1), kind=kCustom, calls=%fused_computation.11 | custom fusion | bytes 1835520 | tf_op jit(solution)/shard_map/scatter | solution.py:38
  81.0 0.0 all-gather.2.cloned.1.call-update
  81.1 172.2 %all-gather.2.cloned.1.call-done = bf16[14336,1024]{1,0:T(8,128)(2,1)} async-done(((bf16[896,1024]{1,0:T(8,128)(2,1)}), bf16[14336,1024]{1,0:T(8,128)(2,1)}) %all-gather.2.cloned.1.call-update) | async-done | bytes 29360144 | tf_op jit(solution)/shard_map/all_gather | solution.py:43
  253.3 31.1 %select_reduce_fusion = f32[896]{0:T(1024)S(1)} fusion(bf16[896,1024]{1,0:T(8,128)(2,1)S(1)} %copy-done, bf16[14336,1024]{1,0:T(8,128)(2,1)} %all-gather.2.cloned.1.call-done, s32[14336]{0:T(1024)S(1)} %fusion.15, s32[896]{0:T(1024)S(1)} %multiply_add_fusion), kind=kOutput, calls=%fused_computation.5 | convolution fusion | flops 26345209856 | bytes 31259648 | tf_op jit(solution)/shard_map/dot_general | solution.py:46
  284.4 3.7 %gather_fusion = f32[896]{0:T(1024)S(1)} fusion(f32[896]{0:T(1024)S(1)} %broadcast_maximum_fusion, s32[1024]{0:T(1024)S(1)} %pad_clamp_fusion.1), kind=kCustom, calls=%fused_computation | custom fusion | bytes 10752 | tf_op jit(solution)/shard_map/gather | solution.py:51
  288.1 0.8 all_to_all.27
  288.9 7.9 %all-to-all-start.2 = ((f32[128,7,1]{1,2,0:T(1,128)}), f32[128,7,1]{1,2,0:T(1,128)S(1)}, u32[]{:S(2)}, u32[]{:S(2)}) async-start(f32[128,7,1]{1,2,0:T(1,128)} %bitcast.5), calls=%async_computation.2 | async-start | bytes 131072 | tf_op jit(solution)/shard_map/all_to_all | solution.py:52
  296.8 9.5 %all-to-all-done.2 = f32[128,7,1]{1,2,0:T(1,128)S(1)} async-done(((f32[128,7,1]{1,2,0:T(1,128)}), f32[128,7,1]{1,2,0:T(1,128)S(1)}, u32[]{:S(2)}, u32[]{:S(2)}) %all-to-all-start.2) | async-done | bytes 3616 | tf_op jit(solution)/shard_map/all_to_all | solution.py:52
  306.3 0.5 broadcast.229
  306.9 0.8 reduce.11
  307.7 0.2 all_to_all.29
  307.9 3.2 %gather_fusion.1 = f32[448]{0:T(512)} fusion(f32[896]{0:T(1024)S(1)} %all_to_all.29, s32[1024]{0:T(1024)S(1)} %pad_clamp_fusion), kind=kCustom, calls=%fused_computation.1 | custom fusion | bytes 5376 | tf_op jit(solution)/shard_map/gather | solution.py:53
  (20 shorter events, 0.2 us)
Async XLA Ops:
  6.5 16.7 %copy-start.2 = (f32[448,8]{0,1:T(8,128)S(1)}, f32[448,8]{0,1:T(8,128)}, u32[]{:S(2)}) copy-start(f32[448,8]{0,1:T(8,128)} %param.5) | copy-start | bytes 43012
  7.7 16.2 %copy-start.1 = (bf16[448,1024]{1,0:T(8,128)(2,1)S(1)}, bf16[448,1024]{1,0:T(8,128)(2,1)}, u32[]{:S(2)}) copy-start(bf16[448,1024]{1,0:T(8,128)(2,1)} %param.4) | copy-start | bytes 2752516
  11.7 21.0 %all-to-all-start = ((s32[128,7,1]{1,2,0:T(1,128)}), s32[128,7,1]{1,2,0:T(1,128)S(1)}, u32[]{:S(2)}, u32[]{:S(2)}) async-start(s32[128,7,1]{1,2,0:T(1,128)} %bitcast.4), calls=%async_computation | async-start | bytes 131072 | tf_op jit(solution)/shard_map/all_to_all | solution.py:34
  32.7 38.9 %all-to-all-start.1 = ((bf16[128,7,1024]{2,1,0:T(8,128)(2,1)}), bf16[128,7,1024]{2,1,0:T(8,128)(2,1)S(1)}, u32[]{:S(2)}, u32[]{:S(2)}) async-start(bf16[128,7,1024]{2,1,0:T(8,128)(2,1)} %all_to_all.24), calls=%async_computation.1 | async-start | bytes 4194304 | tf_op jit(solution)/shard_map/all_to_all | solution.py:33
  42.0 211.4 %all-gather.2.cloned.1.call-start = ((), (), s32[]{:S(2)}) async-start(), calls=%async_computation.3 | async-start | bytes 31195136 | tf_op jit(solution)/shard_map/all_gather | solution.py:43
  81.0 172.3 %copy-start = (bf16[896,1024]{1,0:T(8,128)(2,1)S(1)}, bf16[896,1024]{1,0:T(8,128)(2,1)}, u32[]{:S(2)}) copy-start(bf16[896,1024]{1,0:T(8,128)(2,1)} %scatter_custom_fusion.2) | copy-start | bytes 5505028
  288.9 17.4 %all-to-all-start.2 = ((f32[128,7,1]{1,2,0:T(1,128)}), f32[128,7,1]{1,2,0:T(1,128)S(1)}, u32[]{:S(2)}, u32[]{:S(2)}) async-start(f32[128,7,1]{1,2,0:T(1,128)} %bitcast.5), calls=%async_computation.2 | async-start | bytes 131072 | tf_op jit(solution)/shard_map/all_to_all | solution.py:52
Sparse Core Ops, SparseCore 0:
  81.2 172.1 all-gather.1
where the time goes:
time: 318 us
  waiting for transfers between devices  211 us (66%)
  matrix products  31.1 us (10%)
  starting transfers between devices  28.7 us (9%)
  local copies, waits for them, and re-layouts  26.4 us (8%)
  between operations  13.6 us (4%)
  other arithmetic  6.85 us (2%)
    all_gather x1, waiting for transfers between devices, local(): piece = lax.all_gather(members, 'grp', axis=0, tiled=True)  172 us
    dot_general x1, matrix products, local(): lax.dot_general(members, piece, (((1,), (1,)), ((), ())), preferred_eleme...  31.1 us
    all_to_all x1, waiting for transfers between devices, local(): lax.all_to_all(outgoing, ('row', 'grp'), split_axis=0, concat_axis=0, til...  29.1 us
    all_to_all x1, starting transfers between devices, local(): lax.all_to_all(labels, ('row', 'grp'), split_axis=0, concat_axis=0, tiled...  11.5 us
    all_to_all x1, waiting for transfers between devices, local(): lax.all_to_all(replies, ('row', 'grp'), split_axis=0, concat_axis=0, tile...  9.52 us
    all_to_all x1, starting transfers between devices, local(): lax.all_to_all(outgoing, ('row', 'grp'), split_axis=0, concat_axis=0, til...  9.22 us
    all_to_all x1, starting transfers between devices, local(): lax.all_to_all(replies, ('row', 'grp'), split_axis=0, concat_axis=0, tile...  7.9 us
    scatter x1, local copies, waits for them, and re-layouts, local(): jnp.zeros((slot_count, feature_dim), jnp.bfloat16).at[slot_index]  7.82 us
  transfers between devices with their start and end apart: 4, of which 4 were waited for; matrix products, arithmetic and copies ran while one was open for 2% of the time, Pallas kernels for 0%

commit v1 on v0

v1 whole, which is shorter than its diff:
```python
import functools

import jax
import jax.numpy as jnp
from jax import lax
from jax.experimental import pallas as pl
from jax.experimental.pallas import tpu as pltpu
from jax.sharding import PartitionSpec as P

MESH = pl.DeviceIdType.MESH

OFFSETS = (
    (0, 0, 0), (3, 0, 0), (0, 1, 0), (1, 0, 0), (0, 0, 1), (1, 0, 3), (0, 2, 0), (3, 2, 0), (0, 0, 2), (1, 0, 2),
    (3, 3, 0), (1, 3, 3),
)
SLOTS = len(OFFSETS)
CHUNKS = 7
SORT, ARRIVE, SEND, BEGIN, READY, PAIRS, SHARED, OWN = range(8)
PLAN = (
    (SORT, 0), (SORT, 1), (ARRIVE, 0, 0, 0), (ARRIVE, 1, 0, 0), (SEND, 0, 0, 3, 0), (SEND, 0, 0, 1, 0),
    (SEND, 0, 0, 2, 0), (SEND, 0, 0, 4, 0), (SORT, 2), (ARRIVE, 0, 0, 1), (ARRIVE, 1, 0, 1), (SEND, 1, 0, 3, 0),
    (SEND, 1, 0, 1, 0), (SEND, 1, 0, 2, 0), (SEND, 1, 0, 4, 0), (SORT, 3), (ARRIVE, 0, 0, 2), (ARRIVE, 1, 0, 2),
    (SORT, 4), (ARRIVE, 0, 0, 3), (ARRIVE, 1, 0, 3), (SORT, 5), (ARRIVE, 0, 0, 4), (ARRIVE, 1, 0, 4), (SORT, 6),
    (ARRIVE, 0, 0, 5), (ARRIVE, 1, 0, 5), (ARRIVE, 0, 0, 6), (ARRIVE, 1, 0, 6), (SEND, 0, 0, 3, 1),
    (SEND, 0, 0, 1, 1), (SEND, 0, 0, 2, 1), (SEND, 0, 0, 4, 1), (BEGIN, 0), (READY, 0), (OWN,), (SEND, 1, 0, 3, 1),
    (SEND, 1, 0, 1, 1), (SEND, 1, 0, 2, 1), (SEND, 1, 0, 4, 1), (ARRIVE, 0, 3, 0), (ARRIVE, 0, 1, 0),
    (ARRIVE, 0, 2, 0), (ARRIVE, 0, 4, 0), (SEND, 0, 3, 5, 0), (SEND, 0, 1, 10, 0), (SEND, 0, 0, 3, 2),
    (SEND, 0, 0, 1, 2), (SEND, 0, 0, 2, 2), (SEND, 0, 0, 4, 2), (ARRIVE, 1, 3, 0), (ARRIVE, 1, 1, 0),
    (ARRIVE, 1, 2, 0), (ARRIVE, 1, 4, 0), (SEND, 1, 3, 5, 0), (SEND, 1, 1, 10, 0), (SEND, 1, 0, 3, 2),
    (SEND, 1, 0, 1, 2), (SEND, 1, 0, 2, 2), (SEND, 1, 0, 4, 2), (BEGIN, 1), (BEGIN, 2), (BEGIN, 3), (BEGIN, 4),
    (ARRIVE, 0, 3, 1), (ARRIVE, 0, 1, 1), (ARRIVE, 0, 2, 1), (ARRIVE, 0, 4, 1), (SEND, 0, 3, 5, 1),
    (SEND, 0, 1, 10, 1), (SEND, 0, 0, 3, 3), (SEND, 0, 0, 1, 3), (SEND, 0, 0, 2, 3), (SEND, 0, 0, 4, 3),
    (ARRIVE, 1, 3, 1), (ARRIVE, 1, 1, 1), (ARRIVE, 1, 2, 1), (ARRIVE, 1, 4, 1), (SEND, 1, 3, 5, 1),
    (SEND, 1, 1, 10, 1), (ARRIVE, 0, 5, 0), (ARRIVE, 0, 10, 0), (SEND, 1, 0, 3, 3), (SEND, 1, 0, 1, 3),
    (SEND, 1, 0, 2, 3), (SEND, 1, 0, 4, 3), (SEND, 0, 10, 7, 0), (ARRIVE, 0, 3, 2), (ARRIVE, 0, 1, 2),
    (ARRIVE, 0, 2, 2), (ARRIVE, 0, 4, 2), (SEND, 0, 3, 5, 2), (ARRIVE, 1, 5, 0), (ARRIVE, 1, 10, 0),
    (SEND, 0, 0, 4, 4), (SEND, 1, 0, 3, 4), (SEND, 1, 0, 1, 4), (SEND, 1, 0, 2, 4), (SEND, 1, 10, 7, 0), (BEGIN, 5),
    (BEGIN, 10), (ARRIVE, 1, 3, 2), (ARRIVE, 1, 1, 2), (ARRIVE, 1, 2, 2), (ARRIVE, 1, 4, 2), (SEND, 1, 3, 5, 2),
    (ARRIVE, 0, 5, 1), (ARRIVE, 0, 10, 1), (SEND, 0, 0, 3, 4), (SEND, 0, 0, 1, 4), (SEND, 0, 0, 2, 4),
    (SEND, 1, 0, 4, 4), (SEND, 1, 5, 9, 0), (SEND, 0, 10, 7, 1), (ARRIVE, 0, 3, 3), (ARRIVE, 0, 1, 3),
    (ARRIVE, 0, 2, 3), (ARRIVE, 0, 4, 3), (ARRIVE, 1, 5, 1), (ARRIVE, 1, 10, 1), (SEND, 0, 4, 8, 0),
    (SEND, 1, 0, 3, 5), (SEND, 1, 0, 1, 5), (SEND, 1, 0, 2, 5), (SEND, 1, 10, 7, 1), (SEND, 0, 3, 5, 3),
    (ARRIVE, 1, 3, 3), (ARRIVE, 1, 1, 3), (ARRIVE, 1, 2, 3), (ARRIVE, 1, 4, 3), (ARRIVE, 0, 7, 0), (ARRIVE, 0, 5, 2),
    (SEND, 1, 4, 8, 0), (SEND, 0, 0, 3, 5), (SEND, 0, 0, 1, 5), (SEND, 0, 0, 2, 5), (SEND, 0, 1, 10, 2),
    (SEND, 1, 3, 5, 3), (ARRIVE, 0, 4, 4), (ARRIVE, 1, 3, 4), (ARRIVE, 1, 1, 4), (ARRIVE, 1, 2, 4),
    (ARRIVE, 1, 7, 0), (ARRIVE, 1, 5, 2), (SEND, 0, 7, 6, 0), (SEND, 1, 0, 4, 5), (SEND, 1, 0, 1, 6),
    (SEND, 1, 0, 2, 6), (SEND, 1, 5, 11, 0), (SEND, 0, 5, 9, 1), (BEGIN, 7), (ARRIVE, 0, 3, 4), (ARRIVE, 0, 1, 4),
    (ARRIVE, 0, 2, 4), (ARRIVE, 1, 4, 4), (ARRIVE, 1, 9, 0), (ARRIVE, 0, 7, 1), (SEND, 1, 7, 6, 0),
    (SEND, 0, 0, 4, 5), (SEND, 0, 0, 1, 6), (SEND, 0, 0, 2, 6), (SEND, 1, 3, 5, 4), (ARRIVE, 0, 8, 0),
    (ARRIVE, 1, 3, 5), (ARRIVE, 1, 1, 5), (ARRIVE, 1, 2, 5), (SEND, 1, 1, 10, 5), (ARRIVE, 1, 7, 1),
    (ARRIVE, 0, 5, 3), (SEND, 0, 8, 9, 0), (SEND, 0, 4, 8, 1), (SEND, 1, 2, 6, 2), (SEND, 0, 3, 5, 4),
    (ARRIVE, 1, 8, 0), (ARRIVE, 0, 3, 5), (ARRIVE, 0, 1, 5), (ARRIVE, 0, 2, 5), (SEND, 0, 1, 10, 5),
    (ARRIVE, 0, 10, 2), (ARRIVE, 1, 5, 3), (SEND, 1, 4, 8, 1), (SEND, 0, 2, 6, 3), (SEND, 1, 0, 3, 6),
    (SEND, 0, 5, 9, 2), (SEND, 0, 10, 7, 2), (BEGIN, 8), (ARRIVE, 0, 6, 0), (ARRIVE, 1, 4, 5), (ARRIVE, 1, 1, 6),
    (ARRIVE, 1, 2, 6), (ARRIVE, 1, 11, 0), (ARRIVE, 0, 9, 1), (SEND, 1, 2, 6, 3), (SEND, 0, 0, 3, 6),
    (SEND, 1, 0, 4, 6), (SEND, 0, 5, 11, 0), (SEND, 1, 3, 5, 5), (ARRIVE, 1, 6, 0), (ARRIVE, 0, 4, 5),
    (ARRIVE, 0, 1, 6), (ARRIVE, 0, 2, 6), (ARRIVE, 1, 5, 4), (ARRIVE, 1, 10, 5), (SEND, 1, 7, 6, 1),
    (SEND, 0, 2, 6, 4), (SEND, 0, 0, 4, 6), (SEND, 0, 3, 5, 5), (SEND, 1, 10, 7, 5), (BEGIN, 6), (READY, 1),
    (READY, 2), (ARRIVE, 0, 9, 0), (ARRIVE, 0, 8, 1), (ARRIVE, 1, 6, 2), (SEND, 1, 6, 7, 2), (ARRIVE, 0, 5, 4),
    (ARRIVE, 0, 10, 5), (PAIRS, 2, (0, 1)), (SEND, 0, 7, 6, 1), (SEND, 0, 4, 8, 2), (SEND, 1, 2, 6, 4),
    (SEND, 0, 10, 7, 5), (BEGIN, 9), (ARRIVE, 1, 8, 1), (ARRIVE, 0, 6, 3), (ARRIVE, 1, 3, 6), (SEND, 0, 6, 7, 3),
    (SEND, 1, 3, 5, 6), (ARRIVE, 0, 9, 2), (ARRIVE, 0, 7, 2), (SEND, 1, 8, 9, 1), (SEND, 1, 4, 8, 2),
    (SEND, 0, 2, 6, 6), (SEND, 0, 5, 11, 1), (ARRIVE, 1, 6, 3), (ARRIVE, 0, 3, 6), (ARRIVE, 1, 4, 6),
    (SEND, 1, 6, 7, 3), (SEND, 0, 3, 5, 6), (ARRIVE, 0, 11, 0), (ARRIVE, 1, 5, 5), (PAIRS, 1, (0,)),
    (SEND, 0, 7, 6, 2), (SEND, 0, 4, 8, 3), (SEND, 1, 2, 6, 6), (SEND, 1, 5, 11, 1), (SEND, 0, 5, 9, 4), (BEGIN, 11),
    (READY, 3), (ARRIVE, 1, 6, 1), (ARRIVE, 0, 6, 4), (ARRIVE, 0, 4, 6), (SEND, 0, 6, 7, 4), (ARRIVE, 1, 7, 2),
    (ARRIVE, 0, 5, 5), (ARRIVE, 1, 7, 5), (SEND, 1, 7, 10, 2), (SEND, 1, 4, 8, 3), (SEND, 1, 7, 6, 5),
    (SEND, 0, 5, 11, 2), (SEND, 1, 5, 9, 5), (PAIRS, 3, (2,)), (READY, 4), (ARRIVE, 0, 6, 1), (ARRIVE, 0, 8, 2),
    (ARRIVE, 1, 6, 4), (SEND, 1, 6, 7, 4), (ARRIVE, 0, 7, 3), (ARRIVE, 0, 7, 5), (ARRIVE, 1, 5, 6),
    (SEND, 0, 7, 10, 3), (SEND, 1, 4, 8, 4), (SEND, 0, 7, 6, 5), (SEND, 1, 5, 11, 2), (SEND, 0, 5, 9, 5),
    (PAIRS, 4, (0, 1, 2)), (ARRIVE, 1, 9, 1), (ARRIVE, 1, 8, 2), (ARRIVE, 0, 6, 6), (SEND, 0, 6, 7, 6),
    (ARRIVE, 0, 11, 1), (ARRIVE, 1, 7, 3), (ARRIVE, 0, 5, 6), (SEND, 1, 8, 9, 2), (SEND, 1, 7, 10, 3),
    (SEND, 0, 4, 8, 5), (SEND, 1, 5, 11, 3), (SEND, 1, 5, 9, 6), (ARRIVE, 0, 6, 2), (ARRIVE, 0, 8, 3),
    (ARRIVE, 1, 6, 6), (SEND, 1, 6, 7, 6), (READY, 5), (ARRIVE, 1, 11, 1), (ARRIVE, 0, 9, 4), (ARRIVE, 0, 7, 4),
    (SEND, 0, 8, 9, 3), (SEND, 0, 7, 10, 4), (SEND, 0, 4, 8, 6), (SEND, 0, 5, 11, 3), (SEND, 0, 9, 8, 4),
    (SEND, 0, 5, 9, 6), (ARRIVE, 1, 10, 2), (ARRIVE, 1, 8, 3), (ARRIVE, 1, 6, 5), (ARRIVE, 0, 11, 2),
    (ARRIVE, 1, 7, 4), (ARRIVE, 1, 9, 5), (SEND, 1, 8, 9, 3), (SEND, 1, 7, 10, 4), (SEND, 1, 4, 8, 6),
    (SEND, 1, 5, 11, 4), (SEND, 1, 9, 8, 5), (PAIRS, 5, (0, 1, 2)), (ARRIVE, 0, 10, 3), (ARRIVE, 1, 8, 4),
    (ARRIVE, 0, 6, 5), (ARRIVE, 1, 11, 2), (ARRIVE, 0, 9, 5), (ARRIVE, 0, 7, 6), (SEND, 1, 8, 9, 4),
    (SEND, 0, 7, 10, 6), (SEND, 0, 5, 11, 4), (READY, 6), (ARRIVE, 1, 9, 2), (ARRIVE, 1, 10, 3), (ARRIVE, 0, 8, 5),
    (ARRIVE, 1, 11, 3), (ARRIVE, 1, 9, 6), (ARRIVE, 1, 7, 6), (SEND, 1, 7, 10, 6), (SEND, 1, 5, 11, 5),
    (PAIRS, 6, (1, 4, 5)), (ARRIVE, 0, 9, 3), (ARRIVE, 0, 10, 4), (ARRIVE, 0, 8, 6), (READY, 7), (ARRIVE, 0, 11, 3),
    (ARRIVE, 0, 8, 4), (ARRIVE, 0, 9, 6), (SEND, 0, 5, 11, 5), (ARRIVE, 1, 9, 3), (ARRIVE, 1, 10, 4),
    (ARRIVE, 1, 8, 6), (ARRIVE, 1, 11, 4), (ARRIVE, 1, 8, 5), (SEND, 1, 5, 11, 6), (PAIRS, 7, (4, 5)),
    (ARRIVE, 1, 9, 4), (ARRIVE, 0, 10, 6), (READY, 8), (ARRIVE, 0, 11, 4), (SEND, 0, 5, 11, 6), (READY, 9),
    (ARRIVE, 1, 10, 6), (ARRIVE, 1, 11, 5), (PAIRS, 9, (0, 2, 6)), (READY, 10), (ARRIVE, 0, 11, 5),
    (ARRIVE, 1, 11, 6), (PAIRS, 10, (3, 4, 5)), (ARRIVE, 0, 11, 6), (PAIRS, 10, (8, 9)), (READY, 11),
    (PAIRS, 11, (1, 3, 6)), (PAIRS, 8, (2, 11)), (SHARED, 9, (7,), 0), (SHARED, 9, (3,), 2), (SHARED, 9, (1,), 0),
    (SHARED, 8, (6,), 1), (SHARED, 7, (3,), 0), (SHARED, 7, (1,), 1), (SHARED, 3, (1,), 0),
)

ROWS = 448
WINDOW = 128
CLUSTERS = 8
NONE = 1 << 20


def place():
    row, grp = lax.axis_index("row"), lax.axis_index("grp")
    return grp // 4, row // 2, grp % 4, row % 2


def device(x, y, z, core):
    return (lax.rem(y + 4, 4) * 2 + core, lax.rem(x + 4, 4) * 4 + lax.rem(z + 4, 4))


def scores(left, right):
    return lax.dot_general(
        left, right, (((1,), (1,)), ((), ())), preferred_element_type=jnp.float32
    )


def kernel(emb, scales, cid, rank, out, *refs):
    own, sib = refs[:SLOTS], refs[SLOTS : 2 * SLOTS]
    (
        unit, table, meta_own, meta_sib, first_own, first_sib, col, row_best, col_best, gathered, outgoing, incoming,
        recv, recv_meta, sib_recv, sib_recv_meta, sent, sent_meta, sib_sent, sib_sent_meta, local, back_sent, back_recv,
    ) = refs[2 * SLOTS :]
    x, y, z, core = place()
    chunk_rows = ROWS // CHUNKS
    def other():
        return device(x, y, z, 1 - core)

    barrier = pltpu.get_barrier_semaphore()
    for dx, dy, dz in ((1, 0, 0), (-1, 0, 0), (0, 1, 0), (0, -1, 0), (0, 0, 1), (0, 0, -1)):
        pl.semaphore_signal(
            barrier, inc=1, device_id=device(x + dx, y + dy, z + dz, core), device_id_type=MESH
        )
    pl.semaphore_signal(barrier, inc=1, device_id=other(), device_id_type=MESH)

    def clear(i, _):
        row_best[i] = jnp.full((2 * WINDOW, WINDOW), -1.0, jnp.float32)
        col_best[i] = jnp.full((8, 2 * WINDOW), -1.0, jnp.float32)
        return 0

    lax.fori_loop(0, SLOTS * 4, clear, 0)

    total = jnp.zeros((ROWS, 1), jnp.float32)
    for b in range(8):
        part = emb[:, b * 128 : (b + 1) * 128].astype(jnp.float32) * scales[:, b : b + 1]
        total = total + jnp.sum(part * part, axis=1, keepdims=True)
    inverse = lax.rsqrt(total + 1e-06)
    for b in range(8):
        part = emb[:, b * 128 : (b + 1) * 128].astype(jnp.float32) * scales[:, b : b + 1]
        unit[:, b * 128 : (b + 1) * 128] = (part * inverse).astype(jnp.bfloat16)

    cids, ranks = cid[...], rank[...]
    sub16 = lax.broadcasted_iota(jnp.int32, (16, ROWS), 0)
    member = sub16 == cids
    earlier = (
        lax.broadcasted_iota(jnp.int32, (ROWS, ROWS), 0) < lax.broadcasted_iota(jnp.int32, (ROWS, ROWS), 1)
    )
    before = jnp.dot(
        jnp.where(member, 1.0, 0.0).astype(jnp.bfloat16),
        jnp.where(earlier, 1.0, 0.0).astype(jnp.bfloat16),
        preferred_element_type=jnp.float32,
    )
    sub128 = lax.broadcasted_iota(jnp.int32, (WINDOW, ROWS), 0)
    start = jnp.sum(jnp.where(cids < sub128, 1, 0), axis=1, keepdims=True)
    position = jnp.sum(
        jnp.where(member, before + start[0:16].astype(jnp.float32), 0.0), axis=0, keepdims=True
    ).astype(jnp.int32)
    tile_start = jnp.minimum(start >> 4, (ROWS - WINDOW) // 16)
    window_start = tile_start * 16
    diagonal = lax.broadcasted_iota(jnp.int32, (WINDOW, WINDOW), 0) == lax.broadcasted_iota(
        jnp.int32, (WINDOW, WINDOW), 1
    )
    start_row = jnp.sum(jnp.where(diagonal, tile_start, 0), axis=0, keepdims=True)
    for c in range(CLUSTERS):
        spot = window_start[c : c + 1, :] + lax.broadcasted_iota(jnp.int32, (WINDOW, ROWS), 0)
        hit = jnp.logical_and(spot == position, cids == c)
        table[c * WINDOW : (c + 1) * WINDOW, :] = jnp.where(hit, 1.0, 0.0).astype(jnp.bfloat16)
    digits = jnp.where(
        sub16 == 0, ranks >> 7, jnp.where(sub16 == 1, ranks & 127, jnp.where(sub16 == 2, 1, 0))
    ).astype(jnp.float32).astype(jnp.bfloat16)
    placed = scores(digits, table[...])
    slot_rank = jnp.where(placed[2:3] > 0.5, placed[0:1] * 128.0 + placed[1:2], float(NONE)).astype(jnp.int32)
    meta_own[0] = jnp.concatenate(
        [slot_rank[:, c * WINDOW : (c + 1) * WINDOW] for c in range(CLUSTERS)]
        + [start_row, jnp.zeros((7, WINDOW), jnp.int32)],
        axis=0,
    )

    def sort_chunk(k):
        spot = lax.broadcasted_iota(jnp.int32, (chunk_rows, ROWS), 0) + k * chunk_rows
        move = jnp.where(spot == position, 1.0, 0.0).astype(jnp.bfloat16)
        own[0][k * chunk_rows : (k + 1) * chunk_rows, :] = jnp.dot(
            move, unit[...], preferred_element_type=jnp.float32
        ).astype(jnp.bfloat16)

    def piece(ref, chunk):
        return ref.at[pl.ds(chunk * chunk_rows, chunk_rows)]

    def to_sibling(slot, chunk):
        return pltpu.make_async_remote_copy(
            src_ref=own[slot] if chunk is None else piece(own[slot], chunk),
            dst_ref=sib[slot] if chunk is None else piece(sib[slot], chunk),
            send_sem=sib_sent.at[slot], recv_sem=sib_recv.at[slot],
            device_id=other(), device_id_type=MESH,
        )

    def meta_to_sibling(slot):
        return pltpu.make_async_remote_copy(
            src_ref=meta_own.at[slot], dst_ref=meta_sib.at[slot],
            send_sem=sib_sent_meta.at[slot], recv_sem=sib_recv_meta.at[slot],
            device_id=other(), device_id_type=MESH,
        )

    def target(e, d):
        ux, uy, uz = (q - p for p, q in zip(OFFSETS[e], OFFSETS[d]))
        return device(x - ux, y - uy, z - uz, core)

    def along(e, d, chunk):
        return pltpu.make_async_remote_copy(
            src_ref=own[e] if chunk is None else piece(own[e], chunk),
            dst_ref=own[d] if chunk is None else piece(own[d], chunk),
            send_sem=sent.at[d - 1],
            recv_sem=recv.at[(d - 1) * CHUNKS + (chunk or 0)],
            device_id=target(e, d), device_id_type=MESH,
        )

    def meta_along(e, d):
        return pltpu.make_async_remote_copy(
            src_ref=meta_own.at[e], dst_ref=meta_own.at[d],
            send_sem=sent_meta.at[d - 1], recv_sem=recv_meta.at[d - 1],
            device_id=target(e, d), device_id_type=MESH,
        )

    def starts_to_scalars(slot):
        return [
            pltpu.make_async_copy(meta.at[slot, pl.ds(8, 1)], first.at[slot], local.at[slot * 2 + n])
            for n, (meta, first) in enumerate(((meta_own, first_own), (meta_sib, first_sib)))
        ]

    def arrive(c, slot, chunk):
        if slot == 0:
            if chunk == 0:
                meta_to_sibling(0).start()
        else:
            e = parent_of[(c, slot, chunk)]
            along(e, slot, chunk).wait_recv()
            if chunk == 0:
                meta_along(e, slot).wait_recv()
                meta_to_sibling(slot).start()
        to_sibling(slot, chunk).start()

    def send(c, e, d, chunk):
        if chunk == 0:
            meta_along(e, d).start()
        along(e, d, chunk).start()

    parent_of = {}
    for item in PLAN:
        if item[0] == SEND:
            _, c, e, d, chunk = item
            parent_of[(c, d, chunk)] = e

    def begin(slot):
        meta_to_sibling(slot).wait_recv()
        for copy in starts_to_scalars(slot):
            copy.start()
        for n, meta in enumerate((meta_own, meta_sib)):
            tile = meta[slot, 0:8, :]
            mine = jnp.where(core == 0, tile, jnp.concatenate([tile[4:8], tile[0:4]], axis=0))
            turned = mine.astype(jnp.float32).T
            for q in range(4):
                col[slot * 4 + q, pl.ds(n * WINDOW, WINDOW), :] = jnp.broadcast_to(
                    turned[:, q : q + 1], (WINDOW, WINDOW)
                )

    def ready(slot):
        to_sibling(slot, None).wait_recv()
        for copy in starts_to_scalars(slot):
            copy.wait()

    def window(slot, cluster):
        return [
            ref[pl.ds(first[slot, 0, cluster] * 16, WINDOW), :]
            for ref, first in ((own[slot], first_own), (sib[slot], first_sib))
        ]

    def pairs(b, group, count, base, itself=False):
        def one(i, _):
            q = base + i
            cluster = core * 4 + q
            right = jnp.concatenate(window(b, cluster), axis=0)
            left = jnp.concatenate([w for a in group for w in window(a, cluster)], axis=0)
            found = scores(left, right)
            right_rank = jnp.concatenate(
                [meta[b, pl.ds(cluster, 1), :] for meta in (meta_own, meta_sib)], axis=1
            ).astype(jnp.float32)
            for n, a in enumerate(group):
                value = found[n * 2 * WINDOW : (n + 1) * 2 * WINDOW]
                less = right_rank < jnp.concatenate([col[a * 4 + q]] * 2, axis=1)
                to_left = jnp.where(less, value, -1.0)
                row_best[a * 4 + q] = jnp.maximum(
                    row_best[a * 4 + q], jnp.maximum(to_left[:, :WINDOW], to_left[:, WINDOW:])
                )
                if not itself:
                    to_right = jnp.where(less, -1.0, value).reshape(2 * WINDOW // 8, 8, 2 * WINDOW)
                    col_best[b * 4 + q] = jnp.maximum(col_best[b * 4 + q], jnp.max(to_right, axis=0))
            return 0

        lax.fori_loop(0, count, one, 0, unroll=2)

    def on_core(c, steps):
        @pl.when(core == c)
        def _():
            for step in steps:
                step()

    pending = [[], []]

    def flush():
        for c in (0, 1):
            if pending[c]:
                on_core(c, pending[c])
            pending[c] = []

    pl.semaphore_wait(barrier, 7)
    for item in PLAN:
        if item[0] == ARRIVE:
            pending[item[1]].append(functools.partial(arrive, *item[1:]))
            continue
        if item[0] == SEND:
            pending[item[1]].append(functools.partial(send, *item[1:]))
            continue
        flush()
        if item[0] == SORT:
            sort_chunk(item[1])
        elif item[0] == BEGIN:
            begin(item[1])
        elif item[0] == READY:
            ready(item[1])
        elif item[0] == PAIRS:
            pairs(item[1], item[2], 4, 0)
        elif item[0] == SHARED:
            pairs(item[1], item[2], 2, (x, y, z)[item[3]] // 2 * 2)
        else:
            pairs(0, (0,), 4, 0, itself=True)
    flush()

    lane = lax.broadcasted_iota(jnp.int32, (2 * WINDOW, WINDOW), 1)

    def fold(i, best):
        for q in range(4):
            best = jnp.where(lane == i * 8 + q, jnp.max(row_best[i * 4 + q], axis=1, keepdims=True), best)
            gathered[pl.ds(i * 8 + q, 1), :] = jnp.max(col_best[i * 4 + q], axis=0, keepdims=True)
        for q in range(4, 8):
            gathered[pl.ds(i * 8 + q, 1), :] = jnp.full((1, 2 * WINDOW), -1.0, jnp.float32)
        return best

    best = lax.fori_loop(0, SLOTS, fold, jnp.full((2 * WINDOW, WINDOW), -1.0, jnp.float32))
    turned = best.T
    for n in (0, 1):
        half = jnp.maximum(
            turned[: SLOTS * 8, n * WINDOW : (n + 1) * WINDOW], gathered[:, n * WINDOW : (n + 1) * WINDOW]
        )
        outgoing[n] = half

    def reply(d, n):
        ox, oy, oz = OFFSETS[d]
        return pltpu.make_async_remote_copy(
            src_ref=outgoing.at[n, pl.ds(d * 8, 8)], dst_ref=incoming.at[n, pl.ds(d * 8, 8)],
            send_sem=back_sent.at[d * 2 + n], recv_sem=back_recv.at[d * 2 + n],
            device_id=device(x + ox, y + oy, z + oz, core if n == 0 else 1 - core), device_id_type=MESH,
        )

    replies = [(d, n) for d in range(SLOTS) for n in (0, 1) if d or n]
    for d, n in replies:
        reply(d, n).start()
    for d in range(1, SLOTS):
        along(0, d, None).wait_send()
        meta_along(0, d).wait_send()
    for d in range(SLOTS):
        to_sibling(d, None).wait_send()
        meta_to_sibling(d).wait_send()
    for d, n in replies:
        reply(d, n).wait_recv()
    final = []
    for n in (0, 1):
        best = outgoing[n, 0:8] if n == 0 else incoming[n, 0:8]
        for d in range(1, SLOTS):
            best = jnp.maximum(best, incoming[n, d * 8 : (d + 1) * 8])
        final.append(best)
    lower = jnp.where(core == 0, final[0], final[1])
    upper = jnp.where(core == 0, final[1], final[0])
    line = jnp.concatenate([lower[q : q + 1] for q in range(4)] + [upper[q : q + 1] for q in range(4)], axis=1)
    high = line.astype(jnp.bfloat16)
    rest = line - high.astype(jnp.float32)
    middle = rest.astype(jnp.bfloat16)
    low = (rest - middle.astype(jnp.float32)).astype(jnp.bfloat16)
    sub = lax.broadcasted_iota(jnp.int32, (16, CLUSTERS * WINDOW), 0)
    parts = jnp.where(
        sub == 0, high.astype(jnp.float32),
        jnp.where(sub == 1, middle.astype(jnp.float32), jnp.where(sub == 2, low.astype(jnp.float32), 0.0)),
    ).astype(jnp.bfloat16)
    out[...] = jnp.sum(jnp.dot(parts, table[...], preferred_element_type=jnp.float32), axis=0, keepdims=True)
    for d, n in replies:
        reply(d, n).wait_send()


def local(embeddings, scales, cluster_id, doc_rank):
    vmem = pl.BlockSpec(memory_space=pltpu.VMEM)
    dma = pltpu.SemaphoreType.DMA
    best = pl.pallas_call(
        kernel,
        out_shape=jax.ShapeDtypeStruct((1, ROWS), jnp.float32),
        in_specs=[vmem] * 4,
        out_specs=vmem,
        scratch_shapes=[pltpu.VMEM((ROWS, 1024), jnp.bfloat16)] * (2 * SLOTS)
        + [
            pltpu.VMEM((ROWS, 1024), jnp.bfloat16),
            pltpu.VMEM((CLUSTERS * WINDOW, ROWS), jnp.bfloat16),
            pltpu.VMEM((SLOTS, 16, WINDOW), jnp.int32),
            pltpu.VMEM((SLOTS, 16, WINDOW), jnp.int32),
            pltpu.SMEM((SLOTS, 1, WINDOW), jnp.int32),
            pltpu.SMEM((SLOTS, 1, WINDOW), jnp.int32),
            pltpu.VMEM((SLOTS * 4, 2 * WINDOW, WINDOW), jnp.float32),
            pltpu.VMEM((SLOTS * 4, 2 * WINDOW, WINDOW), jnp.float32),
            pltpu.VMEM((SLOTS * 4, 8, 2 * WINDOW), jnp.float32),
            pltpu.VMEM((SLOTS * 8, 2 * WINDOW), jnp.float32),
            pltpu.VMEM((2, SLOTS * 8, WINDOW), jnp.float32),
            pltpu.VMEM((2, SLOTS * 8, WINDOW), jnp.float32),
            dma(((SLOTS - 1) * CHUNKS,)),
            dma((SLOTS - 1,)),
            dma((SLOTS,)),
            dma((SLOTS,)),
            dma((SLOTS - 1,)),
            dma((SLOTS - 1,)),
            dma((SLOTS,)),
            dma((SLOTS,)),
            dma((2 * SLOTS,)),
            dma((2 * SLOTS,)),
            dma((2 * SLOTS,)),
        ],
        compiler_params=pltpu.CompilerParams(
            collective_id=0, has_side_effects=True, vmem_limit_bytes=56 * 2**20
        ),
        cost_estimate=pl.CostEstimate(flops=30 * 10**9, bytes_accessed=2**20, transcendentals=0),
        name="nearest_in_cluster",
    )(embeddings, scales, cluster_id.reshape(1, ROWS), doc_rank.reshape(1, ROWS))
    return best.reshape(ROWS)


def solution(mesh):
    return jax.shard_map(
        local,
        mesh=mesh,
        in_specs=(P(("row", "grp"), None), P(("row", "grp"), None), P(("row", "grp")), P(("row", "grp"))),
        out_specs=P(("row", "grp")),
        check_vma=False,
    )
```

time: 318 us -> 83.8 us (0.26)
  waiting for transfers between devices: 211 us -> 0 us
  Pallas kernels: 0 us -> 80.8 us
  matrix products: 31.1 us -> 0 us
  starting transfers between devices: 28.7 us -> 0 us
  local copies, waits for them, and re-layouts: 26.4 us -> 2.76 us
  between operations: 13.6 us -> 0.01 us
  other arithmetic: 6.85 us -> 0 us
    all_gather x1 -> x0, waiting for transfers between devices: 172 us -> none  [local(): piece = lax.all_gather(members, 'grp', axis=0, tiled=True)]
    pallas_call x0 -> x1, Pallas kernels: none -> 80.8 us  [local(): pl.pallas_call(kernel, out_shape=jax.ShapeDtypeStruct((1, ROWS), jnp.floa...]
    all_to_all x3 -> x0, waiting for transfers between devices: 39.2 us -> none  [the longest x1 29.1 us: local(): lax.all_to_all(outgoing, ('row', 'grp'), split_axis=0, concat_axis=0, til...]
    dot_general x1 -> x0, matrix products: 31.1 us -> none  [local(): lax.dot_general(members, piece, (((1,), (1,)), ((), ())), preferred_eleme...]
    all_to_all x3 -> x0, starting transfers between devices: 28.6 us -> none  [the longest x1 11.5 us: local(): lax.all_to_all(labels, ('row', 'grp'), split_axis=0, concat_axis=0, tiled...]
    scatter x2 -> x0, local copies, waits for them, and re-layouts: 10.7 us -> none  [the longest x1 7.82 us: local(): jnp.zeros((slot_count, feature_dim), jnp.bfloat16).at[slot_index]]
    all_to_all x6 -> x0, local copies, waits for them, and re-layouts: 7.82 us -> none  [the longest x2 5.47 us: local(): lax.all_to_all(outgoing, ('row', 'grp'), split_axis=0, concat_axis=0, til...]
    gather x2 -> x0, local copies, waits for them, and re-layouts: 6.89 us -> none  [the longest x1 3.67 us: local(): replies = best_sim[jnp.minimum(slot_index, slot_count - 1)]]
  transfers between devices with their start and end apart: 4 -> 0, of which waited for: 4 -> 0; matrix products, arithmetic and copies ran while one was open for 2% -> 0% of each run, Pallas kernels for 0% -> 0%
where the time goes in v1:
time: 83.8 us; the launch traced here: 83.6 us
  Pallas kernels  80.8 us (96%)
  local copies, waits for them, and re-layouts  2.76 us (3%)
    pallas_call x1, Pallas kernels, local(): pl.pallas_call(kernel, out_shape=jax.ShapeDtypeStruct((1, ROWS), jnp.floa...  80.8 us
    unnamed x2, local copies, waits for them, and re-layouts  2.76 us

profile of v1, /device:TPU:1, one launch (start us, length us, event | category | flops | bytes accessed | tf_op | source)
XLA Modules:
  0.0 83.6 jit_solution(10977864754009129204)
XLA Ops:
  0.0 1.5 %copy.5.scales = f32[448,8]{1,0:T(8,128)} copy(f32[448,8]{0,1:T(8,128)} %param.5) | data formatting | bytes 28672 | tf_op args[1]
  1.5 80.8 %nearest_in_cluster.1 = f32[1,448]{1,0:T(1,128)} custom-call(bf16[448,1024]{1,0:T(8,128)(2,1)} %emb.1, f32[448,8]{1,0:T(8,128)} %copy.5.scales, s32[1,448]{1,0:T(1,128)} %bitcast.4, s32[1,448]{1,0:T(1,128)} %bitcast.5), custom_call_target="tpu_custom_call" | custom-call | flops 30000001024 | bytes 1048576 | tf_op jit(solution)/shard_map/nearest_in_cluster/pallas_call | solution.py:406
  82.3 1.2 %copy.7 = f32[448]{0:T(512)} copy(f32[448]{0:T(512)} %bitcast.3) | data formatting | bytes 3584

commit v2 on v1

v2 whole, which is shorter than its diff:
```python
import functools

import jax
import jax.numpy as jnp
from jax import lax
from jax.experimental import pallas as pl
from jax.experimental.pallas import tpu as pltpu
from jax.sharding import PartitionSpec as P

MESH = pl.DeviceIdType.MESH

OFFSETS = (
    (0, 0, 0), (0, 1, 0), (0, 0, 3), (1, 0, 0), (3, 1, 0), (0, 0, 1), (3, 2, 0), (0, 0, 2), (0, 3, 2), (0, 3, 3),
    (2, 0, 0), (2, 2, 0),
)
SLOTS = len(OFFSETS)
ROOTS = (0, 1)
EXTRA = 1
CHUNKS = 7
SORT, ARRIVE, SEND, BEGIN, READY, PAIRS, SHARED, OWN, TABLE, FOLD = range(10)
PLAN = (
    (SORT, 0), (TABLE,), (ARRIVE, 0, 0, 0), (ARRIVE, 1, 1, 0), (SEND, 0, 0, 3, 0), (SEND, 0, 0, 1, 0),
    (SEND, 0, 0, 5, 0), (SEND, 0, 0, 2, 0), (SEND, 1, 1, 0, 0), (SEND, 1, 1, 4, 0), (SORT, 1), (SORT, 2),
    (ARRIVE, 0, 0, 1), (ARRIVE, 1, 1, 1), (SEND, 0, 0, 3, 1), (SEND, 0, 0, 1, 1), (SEND, 0, 0, 5, 1),
    (SEND, 1, 1, 0, 1), (SEND, 1, 1, 4, 1), (SORT, 3), (ARRIVE, 0, 0, 2), (ARRIVE, 1, 1, 2), (SEND, 0, 0, 3, 2),
    (SEND, 0, 0, 1, 2), (SEND, 0, 0, 5, 2), (SEND, 0, 0, 2, 2), (SEND, 1, 1, 0, 2), (SEND, 1, 1, 4, 2), (SORT, 4),
    (ARRIVE, 0, 0, 3), (ARRIVE, 1, 1, 3), (SEND, 0, 0, 2, 3), (SORT, 5), (ARRIVE, 0, 0, 4), (ARRIVE, 1, 1, 4),
    (SORT, 6), (ARRIVE, 0, 0, 5), (ARRIVE, 1, 1, 5), (SEND, 0, 0, 3, 3), (SEND, 0, 0, 1, 3), (SEND, 0, 0, 5, 3),
    (SEND, 1, 1, 0, 3), (SEND, 1, 1, 4, 3), (SEND, 0, 0, 2, 4), (ARRIVE, 0, 0, 6), (ARRIVE, 1, 1, 6),
    (SEND, 0, 0, 1, 4), (SEND, 1, 1, 0, 4), (ARRIVE, 0, 3, 0), (ARRIVE, 0, 1, 0), (ARRIVE, 0, 5, 0),
    (ARRIVE, 0, 2, 0), (ARRIVE, 1, 0, 0), (ARRIVE, 1, 4, 0), (SEND, 0, 1, 4, 0), (SEND, 1, 0, 3, 0),
    (SEND, 1, 0, 5, 0), (SEND, 1, 0, 2, 0), (SEND, 0, 0, 1, 5), (SEND, 1, 1, 0, 5), (ARRIVE, 0, 3, 1),
    (ARRIVE, 0, 1, 1), (ARRIVE, 0, 5, 1), (ARRIVE, 1, 0, 1), (ARRIVE, 1, 4, 1), (ARRIVE, 0, 2, 2),
    (SEND, 0, 1, 4, 1), (SEND, 0, 5, 7, 1), (SEND, 1, 0, 3, 1), (SEND, 1, 0, 2, 1), (SEND, 0, 2, 9, 0),
    (SEND, 1, 4, 6, 0), (SEND, 1, 0, 5, 1), (ARRIVE, 0, 3, 2), (ARRIVE, 0, 1, 2), (ARRIVE, 0, 5, 2),
    (ARRIVE, 1, 0, 2), (ARRIVE, 1, 4, 2), (ARRIVE, 0, 2, 3), (SEND, 0, 1, 4, 2), (SEND, 1, 0, 3, 2),
    (SEND, 1, 0, 2, 2), (BEGIN, 0), (BEGIN, 1), (SEND, 1, 0, 5, 2), (SEND, 0, 0, 1, 6), (SEND, 1, 1, 0, 6),
    (ARRIVE, 0, 3, 3), (ARRIVE, 0, 1, 3), (ARRIVE, 0, 5, 3), (ARRIVE, 1, 0, 3), (ARRIVE, 1, 4, 3), (ARRIVE, 0, 2, 4),
    (SEND, 0, 1, 4, 3), (SEND, 1, 0, 3, 3), (SEND, 1, 0, 2, 3), (SEND, 0, 5, 7, 3), (ARRIVE, 0, 4, 0),
    (ARRIVE, 1, 3, 0), (ARRIVE, 1, 5, 0), (ARRIVE, 1, 2, 0), (ARRIVE, 0, 1, 4), (ARRIVE, 1, 0, 4),
    (SEND, 0, 4, 6, 0), (SEND, 1, 2, 9, 0), (SEND, 0, 1, 4, 4), (SEND, 1, 0, 3, 4), (SEND, 1, 0, 2, 4),
    (SEND, 1, 4, 6, 1), (SEND, 0, 0, 3, 4), (SEND, 1, 1, 4, 4), (ARRIVE, 0, 4, 1), (ARRIVE, 0, 7, 1),
    (ARRIVE, 1, 3, 1), (ARRIVE, 1, 2, 1), (ARRIVE, 0, 1, 5), (ARRIVE, 1, 0, 5), (SEND, 0, 7, 2, 1),
    (SEND, 1, 2, 9, 1), (SEND, 1, 0, 2, 5), (SEND, 0, 4, 6, 1), (SEND, 0, 7, 8, 1), (SEND, 1, 0, 5, 3),
    (SEND, 0, 0, 2, 5), (SEND, 0, 1, 4, 5), (SEND, 1, 0, 3, 5), (ARRIVE, 0, 9, 0), (ARRIVE, 1, 6, 0),
    (ARRIVE, 1, 5, 1), (ARRIVE, 0, 4, 2), (ARRIVE, 1, 3, 2), (ARRIVE, 1, 2, 2), (BEGIN, 3), (BEGIN, 4),
    (SEND, 0, 4, 6, 2), (SEND, 0, 0, 3, 5), (SEND, 1, 1, 4, 5), (ARRIVE, 1, 5, 2), (ARRIVE, 0, 4, 3),
    (ARRIVE, 1, 3, 3), (ARRIVE, 1, 2, 3), (ARRIVE, 0, 1, 6), (ARRIVE, 1, 0, 6), (SEND, 1, 5, 7, 2),
    (SEND, 1, 2, 9, 3), (SEND, 1, 0, 2, 6), (BEGIN, 5), (SEND, 1, 4, 6, 2), (SEND, 0, 2, 9, 3), (SEND, 1, 0, 5, 4),
    (SEND, 0, 0, 3, 6), (SEND, 0, 0, 2, 6), (SEND, 1, 1, 4, 6), (READY, 0), (READY, 1), (ARRIVE, 0, 6, 0),
    (ARRIVE, 1, 9, 0), (ARRIVE, 0, 7, 3), (ARRIVE, 0, 4, 4), (ARRIVE, 1, 3, 4), (ARRIVE, 1, 2, 4),
    (SEND, 1, 2, 7, 0), (SEND, 1, 4, 6, 3), (SEND, 0, 0, 5, 4), (SEND, 0, 1, 4, 6), (SEND, 1, 0, 3, 6), (OWN, 0),
    (PAIRS, 1, (0,)), (ARRIVE, 0, 2, 1), (ARRIVE, 1, 9, 1), (ARRIVE, 1, 6, 1), (ARRIVE, 0, 3, 4), (ARRIVE, 1, 4, 4),
    (ARRIVE, 1, 2, 5), (SEND, 0, 2, 9, 1), (SEND, 0, 3, 10, 0), (SEND, 1, 6, 11, 0), (SEND, 1, 2, 7, 1),
    (SEND, 0, 4, 6, 3), (SEND, 1, 2, 9, 4), (SEND, 0, 0, 5, 5), (ARRIVE, 0, 6, 1), (ARRIVE, 0, 8, 1),
    (ARRIVE, 1, 5, 3), (ARRIVE, 0, 2, 5), (ARRIVE, 0, 4, 5), (ARRIVE, 1, 3, 5), (BEGIN, 2), (SEND, 0, 6, 11, 0),
    (SEND, 1, 3, 10, 0), (SEND, 0, 2, 7, 2), (SEND, 1, 4, 6, 4), (SEND, 1, 0, 5, 5), (ARRIVE, 0, 6, 2),
    (ARRIVE, 1, 7, 2), (ARRIVE, 1, 9, 3), (ARRIVE, 0, 3, 5), (ARRIVE, 1, 4, 5), (ARRIVE, 1, 2, 6),
    (SEND, 1, 7, 8, 2), (BEGIN, 6), (SEND, 0, 3, 10, 1), (SEND, 1, 6, 11, 1), (SEND, 1, 2, 7, 3), (SEND, 0, 4, 6, 4),
    (SEND, 1, 2, 9, 5), (SEND, 0, 0, 5, 6), (ARRIVE, 1, 6, 2), (ARRIVE, 0, 9, 3), (ARRIVE, 1, 5, 4),
    (ARRIVE, 0, 3, 6), (ARRIVE, 0, 2, 6), (ARRIVE, 1, 4, 6), (SEND, 1, 9, 8, 0), (SEND, 0, 6, 11, 1),
    (SEND, 1, 3, 10, 1), (SEND, 1, 4, 6, 5), (SEND, 0, 2, 9, 6), (SEND, 1, 0, 5, 6), (READY, 2), (PAIRS, 2, (0, 1)),
    (ARRIVE, 1, 7, 0), (ARRIVE, 0, 9, 1), (ARRIVE, 1, 6, 3), (ARRIVE, 0, 5, 4), (ARRIVE, 0, 4, 6), (ARRIVE, 1, 3, 6),
    (SEND, 0, 9, 8, 0), (SEND, 0, 6, 11, 2), (SEND, 1, 3, 10, 2), (SEND, 0, 4, 6, 5), (READY, 3), (READY, 4),
    (ARRIVE, 0, 10, 0), (ARRIVE, 1, 11, 0), (ARRIVE, 1, 7, 1), (ARRIVE, 0, 6, 3), (ARRIVE, 1, 9, 4),
    (ARRIVE, 0, 5, 5), (SEND, 1, 7, 8, 1), (SEND, 0, 5, 7, 5), (BEGIN, 9), (SEND, 0, 3, 10, 2), (SEND, 1, 6, 11, 2),
    (SEND, 0, 2, 7, 4), (SEND, 0, 4, 6, 6), (PAIRS, 4, (0, 1, 2)), (ARRIVE, 0, 11, 0), (ARRIVE, 1, 10, 0),
    (ARRIVE, 0, 7, 2), (ARRIVE, 1, 8, 2), (ARRIVE, 1, 6, 4), (ARRIVE, 1, 5, 5), (SEND, 0, 7, 8, 2),
    (SEND, 1, 8, 9, 2), (BEGIN, 7), (SEND, 0, 3, 10, 3), (SEND, 1, 6, 11, 3), (SEND, 1, 2, 7, 4), (SEND, 1, 2, 9, 6),
    (SEND, 1, 4, 6, 6), (ARRIVE, 0, 10, 1), (ARRIVE, 1, 11, 1), (ARRIVE, 1, 7, 3), (ARRIVE, 0, 6, 4),
    (ARRIVE, 1, 9, 5), (ARRIVE, 0, 5, 6), (SEND, 0, 5, 7, 6), (SEND, 0, 6, 11, 3), (SEND, 1, 3, 10, 3),
    (SEND, 1, 2, 7, 5), (PAIRS, 3, (2, 4)), (ARRIVE, 1, 8, 0), (ARRIVE, 0, 11, 1), (ARRIVE, 1, 10, 1),
    (ARRIVE, 1, 6, 5), (ARRIVE, 0, 9, 6), (ARRIVE, 1, 5, 6), (SEND, 1, 5, 7, 6), (SEND, 0, 9, 8, 3),
    (SEND, 0, 3, 10, 4), (SEND, 1, 6, 11, 4), (READY, 5), (ARRIVE, 0, 8, 0), (ARRIVE, 1, 8, 1), (ARRIVE, 0, 11, 2),
    (ARRIVE, 1, 10, 2), (ARRIVE, 0, 7, 5), (ARRIVE, 0, 6, 5), (SEND, 0, 8, 7, 0), (SEND, 0, 7, 8, 5), (BEGIN, 10),
    (BEGIN, 11), (SEND, 1, 9, 8, 3), (SEND, 0, 6, 11, 4), (SEND, 1, 3, 10, 4), (PAIRS, 5, (1, 3, 4)),
    (ARRIVE, 0, 10, 2), (ARRIVE, 0, 8, 2), (ARRIVE, 1, 9, 2), (ARRIVE, 1, 11, 2), (ARRIVE, 0, 7, 4),
    (ARRIVE, 0, 6, 6), (SEND, 0, 8, 9, 2), (SEND, 0, 7, 8, 4), (BEGIN, 8), (SEND, 1, 9, 8, 4), (SEND, 0, 3, 10, 5),
    (SEND, 1, 6, 11, 5), (ARRIVE, 0, 10, 3), (ARRIVE, 1, 11, 3), (ARRIVE, 1, 7, 4), (ARRIVE, 0, 7, 6),
    (ARRIVE, 1, 9, 6), (ARRIVE, 1, 6, 6), (SEND, 0, 7, 8, 6), (SEND, 0, 6, 11, 5), (SEND, 1, 3, 10, 5),
    (SEND, 1, 9, 8, 6), (READY, 6), (ARRIVE, 0, 11, 3), (ARRIVE, 1, 10, 3), (ARRIVE, 1, 7, 5), (ARRIVE, 1, 7, 6),
    (SEND, 1, 7, 8, 5), (SEND, 0, 3, 10, 6), (SEND, 1, 6, 11, 6), (PAIRS, 6, (0, 2, 5)), (FOLD, (5,)),
    (ARRIVE, 0, 7, 0), (ARRIVE, 0, 8, 5), (SEND, 0, 8, 9, 5), (ARRIVE, 0, 8, 3), (ARRIVE, 0, 10, 4),
    (ARRIVE, 1, 11, 4), (SEND, 0, 6, 11, 6), (SEND, 1, 3, 10, 6), (READY, 7), (ARRIVE, 0, 9, 2), (ARRIVE, 0, 8, 4),
    (SEND, 0, 8, 9, 4), (ARRIVE, 1, 8, 3), (ARRIVE, 0, 11, 4), (ARRIVE, 1, 10, 4), (PAIRS, 7, (1, 3, 4)),
    (ARRIVE, 0, 8, 6), (ARRIVE, 1, 8, 4), (ARRIVE, 0, 10, 5), (ARRIVE, 1, 11, 5), (PAIRS, 7, (6,)),
    (ARRIVE, 1, 8, 5), (ARRIVE, 0, 11, 5), (ARRIVE, 1, 10, 5), (ARRIVE, 1, 8, 6), (SHARED, 7, (0,), 2),
    (ARRIVE, 0, 9, 5), (SHARED, 6, (3,), 0), (READY, 8), (ARRIVE, 0, 10, 6), (ARRIVE, 1, 11, 6), (PAIRS, 8, (3,)),
    (ARRIVE, 0, 9, 4), (SHARED, 8, (1,), 1), (ARRIVE, 0, 11, 6), (ARRIVE, 1, 10, 6), (READY, 9),
    (PAIRS, 9, (1, 3, 6)), (FOLD, (1, 3, 6)), (READY, 10), (READY, 11), (PAIRS, 11, (2, 8, 9)), (FOLD, (8,)),
    (PAIRS, 10, (2, 4, 9)), (FOLD, (2, 4, 9)), (SHARED, 11, (10,), 1), (SHARED, 11, (7,), 0), (FOLD, (11,)),
    (SHARED, 10, (7,), 0), (FOLD, (7,)), (SHARED, 10, (0,), 0), (FOLD, (0, 10)),
)

ROWS = 448
WINDOW = 128
CLUSTERS = 8
NONE = 1 << 20


def place():
    row, grp = lax.axis_index("row"), lax.axis_index("grp")
    return grp // 4, row // 2, grp % 4, row % 2


def device(x, y, z, core):
    return (lax.rem(y + 4, 4) * 2 + core, lax.rem(x + 4, 4) * 4 + lax.rem(z + 4, 4))


def scores(left, right):
    return lax.dot_general(
        left, right, (((1,), (1,)), ((), ())), preferred_element_type=jnp.float32
    )


def kernel(emb, scales, cid, rank, out, *refs):
    own, sib = refs[:SLOTS], refs[SLOTS : 2 * SLOTS]
    (
        unit, table, meta_own, meta_sib, first_own, first_sib, col, row_best, col_best, outgoing, incoming,
        recv, recv_meta, sib_recv, sib_recv_meta, sent, sent_meta, sib_sent, sib_sent_meta, local, back_sent, back_recv,
    ) = refs[2 * SLOTS :]
    x, y, z, core = place()
    root = ROOTS[0] + core * (ROOTS[1] - ROOTS[0])
    chunk_rows = ROWS // CHUNKS
    def other():
        return device(x, y, z, 1 - core)

    barrier = pltpu.get_barrier_semaphore()
    for dx, dy, dz in ((1, 0, 0), (-1, 0, 0), (0, 1, 0), (0, -1, 0), (0, 0, 1), (0, 0, -1)):
        pl.semaphore_signal(
            barrier, inc=1, device_id=device(x + dx, y + dy, z + dz, core), device_id_type=MESH
        )
    pl.semaphore_signal(barrier, inc=1, device_id=other(), device_id_type=MESH)

    def clear(i, _):
        row_best[i] = jnp.full((2 * WINDOW, WINDOW), -1.0, jnp.float32)
        col_best[i] = jnp.full((8, 2 * WINDOW), -1.0, jnp.float32)
        return 0

    lax.fori_loop(0, SLOTS * 4, clear, 0)

    factor = scales[...].T
    total = jnp.zeros((ROWS, 1), jnp.float32)
    for b in range(8):
        part = emb[:, b * 128 : (b + 1) * 128].astype(jnp.float32) * factor[:, b : b + 1]
        total = total + jnp.sum(part * part, axis=1, keepdims=True)
    inverse = lax.rsqrt(total + 1e-06)
    for b in range(8):
        part = emb[:, b * 128 : (b + 1) * 128].astype(jnp.float32) * factor[:, b : b + 1]
        unit[:, b * 128 : (b + 1) * 128] = (part * inverse).astype(jnp.bfloat16)

    cids, ranks = cid[...], rank[...]
    sub16 = lax.broadcasted_iota(jnp.int32, (16, ROWS), 0)
    member = sub16 == cids
    earlier = (
        lax.broadcasted_iota(jnp.int32, (ROWS, ROWS), 0) < lax.broadcasted_iota(jnp.int32, (ROWS, ROWS), 1)
    )
    before = jnp.dot(
        jnp.where(member, 1.0, 0.0).astype(jnp.bfloat16),
        jnp.where(earlier, 1.0, 0.0).astype(jnp.bfloat16),
        preferred_element_type=jnp.float32,
    )
    sub128 = lax.broadcasted_iota(jnp.int32, (WINDOW, ROWS), 0)
    start = jnp.sum(jnp.where(cids < sub128, 1, 0), axis=1, keepdims=True)
    position = jnp.sum(
        jnp.where(member, before + start[0:16].astype(jnp.float32), 0.0), axis=0, keepdims=True
    ).astype(jnp.int32)
    tile_start = jnp.minimum(start >> 4, (ROWS - WINDOW) // 16)
    window_start = tile_start * 16
    diagonal = lax.broadcasted_iota(jnp.int32, (WINDOW, WINDOW), 0) == lax.broadcasted_iota(
        jnp.int32, (WINDOW, WINDOW), 1
    )
    start_row = jnp.sum(jnp.where(diagonal, tile_start, 0), axis=0, keepdims=True)
    def make_table():
        for c in range(CLUSTERS):
            spot = window_start[c : c + 1, :] + lax.broadcasted_iota(jnp.int32, (WINDOW, ROWS), 0)
            hit = jnp.logical_and(spot == position, cids == c)
            table[c * WINDOW : (c + 1) * WINDOW, :] = jnp.where(hit, 1.0, 0.0).astype(jnp.bfloat16)
        digits = jnp.where(
            sub16 == 0, ranks >> 7, jnp.where(sub16 == 1, ranks & 127, jnp.where(sub16 == 2, 1, 0))
        ).astype(jnp.float32).astype(jnp.bfloat16)
        placed = scores(digits, table[...])
        slot_rank = jnp.where(placed[2:3] > 0.5, placed[0:1] * 128.0 + placed[1:2], float(NONE)).astype(jnp.int32)
        meta_own[root] = jnp.concatenate(
            [slot_rank[:, c * WINDOW : (c + 1) * WINDOW] for c in range(CLUSTERS)]
            + [start_row, jnp.zeros((7, WINDOW), jnp.int32)],
            axis=0,
        )

    def sort_chunk(k):
        spot = lax.broadcasted_iota(jnp.int32, (chunk_rows, ROWS), 0) + k * chunk_rows
        move = jnp.where(spot == position, 1.0, 0.0).astype(jnp.bfloat16)
        rows = jnp.dot(move, unit[...], preferred_element_type=jnp.float32).astype(jnp.bfloat16)
        for c in (0, 1):

            @pl.when(core == c)
            def _():
                own[ROOTS[c]][k * chunk_rows : (k + 1) * chunk_rows, :] = rows

    def piece(ref, chunk):
        return ref.at[pl.ds(chunk * chunk_rows, chunk_rows)]

    def to_sibling(slot, chunk):
        return pltpu.make_async_remote_copy(
            src_ref=own[slot] if chunk is None else piece(own[slot], chunk),
            dst_ref=sib[slot] if chunk is None else piece(sib[slot], chunk),
            send_sem=sib_sent.at[slot], recv_sem=sib_recv.at[slot],
            device_id=other(), device_id_type=MESH,
        )

    def meta_to_sibling(slot):
        return pltpu.make_async_remote_copy(
            src_ref=meta_own.at[slot], dst_ref=meta_sib.at[slot],
            send_sem=sib_sent_meta.at[slot], recv_sem=sib_recv_meta.at[slot],
            device_id=other(), device_id_type=MESH,
        )

    def target(e, d):
        ux, uy, uz = (q - p for p, q in zip(OFFSETS[e], OFFSETS[d]))
        return device(x - ux, y - uy, z - uz, core)

    def along(e, d, chunk):
        return pltpu.make_async_remote_copy(
            src_ref=own[e] if chunk is None else piece(own[e], chunk),
            dst_ref=own[d] if chunk is None else piece(own[d], chunk),
            send_sem=sent.at[d],
            recv_sem=recv.at[d * CHUNKS + (chunk or 0)],
            device_id=target(e, d), device_id_type=MESH,
        )

    def meta_along(e, d):
        return pltpu.make_async_remote_copy(
            src_ref=meta_own.at[e], dst_ref=meta_own.at[d],
            send_sem=sent_meta.at[d], recv_sem=recv_meta.at[d],
            device_id=target(e, d), device_id_type=MESH,
        )

    def starts_to_scalars(slot):
        return [
            pltpu.make_async_copy(meta.at[slot, pl.ds(8, 1)], first.at[slot], local.at[slot * 2 + n])
            for n, (meta, first) in enumerate(((meta_own, first_own), (meta_sib, first_sib)))
        ]

    def arrive(c, slot, chunk):
        if slot != ROOTS[c]:
            e = parent_of[(c, slot, chunk)]
            along(e, slot, chunk).wait_recv()
            if chunk == EXTRA:
                meta_along(e, slot).wait_recv()
        if chunk == EXTRA:
            meta_to_sibling(slot).start()
        to_sibling(slot, chunk).start()

    def send(c, e, d, chunk):
        if chunk == EXTRA:
            meta_along(e, d).start()
        along(e, d, chunk).start()

    parent_of = {}
    for item in PLAN:
        if item[0] == SEND:
            _, c, e, d, chunk = item
            parent_of[(c, d, chunk)] = e

    def begin(slot):
        meta_to_sibling(slot).wait_recv()
        for copy in starts_to_scalars(slot):
            copy.start()
        for n, meta in enumerate((meta_own, meta_sib)):
            tile = meta[slot, 0:8, :]
            mine = jnp.where(core == 0, tile, jnp.concatenate([tile[4:8], tile[0:4]], axis=0))
            turned = mine.astype(jnp.float32).T
            for q in range(4):
                col[slot * 4 + q, pl.ds(n * WINDOW, WINDOW), :] = jnp.broadcast_to(
                    turned[:, q : q + 1], (WINDOW, WINDOW)
                )

    def ready(slot):
        to_sibling(slot, None).wait_recv()
        for copy in starts_to_scalars(slot):
            copy.wait()

    def window(slot, cluster):
        return [
            ref[pl.ds(first[slot, 0, cluster] * 16, WINDOW), :]
            for ref, first in ((own[slot], first_own), (sib[slot], first_sib))
        ]

    def pairs(b, group, count, base, itself=False):
        def one(i, _):
            q = base + i
            cluster = core * 4 + q
            right = jnp.concatenate(window(b, cluster), axis=0)
            left = jnp.concatenate([w for a in group for w in window(a, cluster)], axis=0)
            found = scores(left, right)
            right_rank = jnp.concatenate(
                [meta[b, pl.ds(cluster, 1), :] for meta in (meta_own, meta_sib)], axis=1
            ).astype(jnp.float32)
            for n, a in enumerate(group):
                value = found[n * 2 * WINDOW : (n + 1) * 2 * WINDOW]
                less = right_rank < jnp.concatenate([col[a * 4 + q]] * 2, axis=1)
                to_left = jnp.where(less, value, -1.0)
                row_best[a * 4 + q] = jnp.maximum(
                    row_best[a * 4 + q], jnp.maximum(to_left[:, :WINDOW], to_left[:, WINDOW:])
                )
                if not itself:
                    to_right = jnp.where(less, -1.0, value).reshape(2 * WINDOW // 8, 8, 2 * WINDOW)
                    col_best[b * 4 + q] = jnp.maximum(col_best[b * 4 + q], jnp.max(to_right, axis=0))
            return 0

        lax.fori_loop(0, count, one, 0, unroll=4)

    def on_core(c, steps):
        @pl.when(core == c)
        def _():
            for step in steps:
                step()

    def sent_to(d):
        along((d + 1) % SLOTS, d, None).wait_send()
        meta_along((d + 1) % SLOTS, d).wait_send()

    def reply(d, n):
        away = [[q - p for p, q in zip(OFFSETS[ROOTS[c]], OFFSETS[d])] for c in (n, 1 - n)]
        ox, oy, oz = (first + core * (second - first) for first, second in zip(*away))
        return pltpu.make_async_remote_copy(
            src_ref=outgoing.at[n * SLOTS + d], dst_ref=incoming.at[n * SLOTS + d],
            send_sem=back_sent.at[d * 2 + n], recv_sem=back_recv.at[d * 2 + n],
            device_id=device(x + ox, y + oy, z + oz, core if n == 0 else 1 - core), device_id_type=MESH,
        )

    def replies(d, what):
        if d not in ROOTS:
            getattr(reply(d, 0), what)()
        elif ROOTS[0] != ROOTS[1]:
            on_core(1 - ROOTS.index(d), [getattr(reply(d, 0), what)])
        getattr(reply(d, 1), what)()

    lane = lax.broadcasted_iota(jnp.int32, (2 * WINDOW, WINDOW), 1)

    def fold(group):
        best = jnp.full((2 * WINDOW, WINDOW), -1.0, jnp.float32)
        for n, d in enumerate(group):
            for q in range(4):
                best = jnp.where(lane == n * 8 + q, jnp.max(row_best[d * 4 + q], axis=1, keepdims=True), best)
        turned = best.T
        for n, d in enumerate(group):
            rows = jnp.concatenate(
                [jnp.max(col_best[d * 4 + q], axis=0, keepdims=True) for q in range(4)]
                + [jnp.full((4, 2 * WINDOW), -1.0, jnp.float32)],
                axis=0,
            )
            rows = jnp.maximum(rows, turned[n * 8 : (n + 1) * 8])
            for half in (0, 1):
                outgoing[half * SLOTS + d] = rows[:, half * WINDOW : (half + 1) * WINDOW]
            replies(d, "start")

    pending = [[], []]

    def flush():
        for c in (0, 1):
            if pending[c]:
                on_core(c, pending[c])
            pending[c] = []

    pl.semaphore_wait(barrier, 7)
    for item in PLAN:
        if item[0] == ARRIVE:
            pending[item[1]].append(functools.partial(arrive, *item[1:]))
            continue
        if item[0] == SEND:
            pending[item[1]].append(functools.partial(send, *item[1:]))
            continue
        flush()
        if item[0] == SORT:
            sort_chunk(item[1])
        elif item[0] == TABLE:
            make_table()
        elif item[0] == BEGIN:
            begin(item[1])
        elif item[0] == READY:
            ready(item[1])
        elif item[0] == PAIRS:
            pairs(item[1], item[2], 4, 0)
        elif item[0] == SHARED:
            pairs(item[1], item[2], 2, (x, y, z)[item[3]] // 2 * 2)
        elif item[0] == FOLD:
            fold(item[1])
        else:
            pairs(item[1], (item[1],), 4, 0, itself=True)
    flush()

    for d in range(SLOTS):
        to_sibling(d, None).wait_send()
        meta_to_sibling(d).wait_send()
        if d not in ROOTS:
            sent_to(d)
        elif ROOTS[0] != ROOTS[1]:
            on_core(1 - ROOTS.index(d), [functools.partial(sent_to, d)])
    for d in range(SLOTS):
        replies(d, "wait_recv")
    incoming[root] = outgoing[root]
    final = []
    for n in (0, 1):
        best = incoming[n * SLOTS]
        for d in range(1, SLOTS):
            best = jnp.maximum(best, incoming[n * SLOTS + d])
        final.append(best)
    lower = jnp.where(core == 0, final[0], final[1])
    upper = jnp.where(core == 0, final[1], final[0])
    line = jnp.concatenate([lower[q : q + 1] for q in range(4)] + [upper[q : q + 1] for q in range(4)], axis=1)
    high = line.astype(jnp.bfloat16)
    rest = line - high.astype(jnp.float32)
    middle = rest.astype(jnp.bfloat16)
    low = (rest - middle.astype(jnp.float32)).astype(jnp.bfloat16)
    sub = lax.broadcasted_iota(jnp.int32, (16, CLUSTERS * WINDOW), 0)
    parts = jnp.where(
        sub == 0, high.astype(jnp.float32),
        jnp.where(sub == 1, middle.astype(jnp.float32), jnp.where(sub == 2, low.astype(jnp.float32), 0.0)),
    ).astype(jnp.bfloat16)
    out[...] = jnp.sum(jnp.dot(parts, table[...], preferred_element_type=jnp.float32), axis=0, keepdims=True)
    for d in range(SLOTS):
        replies(d, "wait_send")


def local(embeddings, scales, cluster_id, doc_rank):
    vmem = pl.BlockSpec(memory_space=pltpu.VMEM)
    dma = pltpu.SemaphoreType.DMA
    best = pl.pallas_call(
        kernel,
        out_shape=jax.ShapeDtypeStruct((1, ROWS), jnp.float32),
        in_specs=[vmem] * 4,
        out_specs=vmem,
        scratch_shapes=[pltpu.VMEM((ROWS, 1024), jnp.bfloat16)] * (2 * SLOTS)
        + [
            pltpu.VMEM((ROWS, 1024), jnp.bfloat16),
            pltpu.VMEM((CLUSTERS * WINDOW, ROWS), jnp.bfloat16),
            pltpu.VMEM((SLOTS, 16, WINDOW), jnp.int32),
            pltpu.VMEM((SLOTS, 16, WINDOW), jnp.int32),
            pltpu.SMEM((SLOTS, 1, WINDOW), jnp.int32),
            pltpu.SMEM((SLOTS, 1, WINDOW), jnp.int32),
            pltpu.VMEM((SLOTS * 4, 2 * WINDOW, WINDOW), jnp.float32),
            pltpu.VMEM((SLOTS * 4, 2 * WINDOW, WINDOW), jnp.float32),
            pltpu.VMEM((SLOTS * 4, 8, 2 * WINDOW), jnp.float32),
            pltpu.VMEM((2 * SLOTS, 8, WINDOW), jnp.float32),
            pltpu.VMEM((2 * SLOTS, 8, WINDOW), jnp.float32),
            dma((SLOTS * CHUNKS,)),
            dma((SLOTS,)),
            dma((SLOTS,)),
            dma((SLOTS,)),
            dma((SLOTS,)),
            dma((SLOTS,)),
            dma((SLOTS,)),
            dma((SLOTS,)),
            dma((2 * SLOTS,)),
            dma((2 * SLOTS,)),
            dma((2 * SLOTS,)),
        ],
        compiler_params=pltpu.CompilerParams(
            collective_id=0, has_side_effects=True, vmem_limit_bytes=56 * 2**20
        ),
        cost_estimate=pl.CostEstimate(flops=30 * 10**9, bytes_accessed=2**20, transcendentals=0),
        name="nearest_in_cluster",
    )(embeddings, scales.T, cluster_id.reshape(1, ROWS), doc_rank.reshape(1, ROWS))
    return best.reshape(ROWS)


def solution(mesh):
    return jax.shard_map(
        local,
        mesh=mesh,
        in_specs=(P(("row", "grp"), None), P(("row", "grp"), None), P(("row", "grp")), P(("row", "grp"))),
        out_specs=P(("row", "grp")),
        check_vma=False,
    )
```

time: 83.8 us -> 74.6 us (0.89)
  Pallas kernels: 80.8 us -> 73.2 us
  local copies, waits for them, and re-layouts: 2.76 us -> 1.26 us
    pallas_call x1, Pallas kernels: 80.8 us -> 73.2 us  [local(): pl.pallas_call(kernel, out_shape=jax.ShapeDtypeStruct((1, ROWS), jnp.floa...]
    unnamed x2 -> x1, local copies, waits for them, and re-layouts: 2.76 us -> 1.26 us
where the time goes in v2:
time: 74.6 us; the launch traced here: 74.4 us
  Pallas kernels  73.2 us (98%)
  local copies, waits for them, and re-layouts  1.26 us (2%)
    pallas_call x1, Pallas kernels, local(): pl.pallas_call(kernel, out_shape=jax.ShapeDtypeStruct((1, ROWS), jnp.floa...  73.2 us

profile of v2, /device:TPU:1, one launch (start us, length us, event | category | flops | bytes accessed | tf_op | source)
XLA Modules:
  0.0 74.4 jit_solution(10498527887472959582)
XLA Ops:
  0.0 73.2 %nearest_in_cluster.1 = f32[1,448]{1,0:T(1,128)} custom-call(bf16[448,1024]{1,0:T(8,128)(2,1)} %emb.1, f32[8,448]{1,0:T(8,128)} %bitcast.5, s32[1,448]{1,0:T(1,128)} %bitcast.6, s32[1,448]{1,0:T(1,128)} %bitcast.7), custom_call_target="tpu_custom_call" | custom-call | flops 30000001024 | bytes 1048576 | tf_op jit(solution)/shard_map/nearest_in_cluster/pallas_call | solution.py:429
  73.2 1.3 %copy.6 = f32[448]{0:T(512)} copy(f32[448]{0:T(512)} %bitcast.4) | data formatting | bytes 3584

commit v3 on v2

--- a/solution.py
+++ b/solution.py
@@ -15,14 +15,14 @@
 )
 SLOTS = len(OFFSETS)
 ROOTS = (0, 1)
-EXTRA = 1
+EXTRA = 2
 CHUNKS = 7
 SORT, ARRIVE, SEND, BEGIN, READY, PAIRS, SHARED, OWN, TABLE, FOLD = range(10)
 PLAN = (
-    (SORT, 0), (TABLE,), (ARRIVE, 0, 0, 0), (ARRIVE, 1, 1, 0), (SEND, 0, 0, 3, 0), (SEND, 0, 0, 1, 0),
-    (SEND, 0, 0, 5, 0), (SEND, 0, 0, 2, 0), (SEND, 1, 1, 0, 0), (SEND, 1, 1, 4, 0), (SORT, 1), (SORT, 2),
-    (ARRIVE, 0, 0, 1), (ARRIVE, 1, 1, 1), (SEND, 0, 0, 3, 1), (SEND, 0, 0, 1, 1), (SEND, 0, 0, 5, 1),
-    (SEND, 1, 1, 0, 1), (SEND, 1, 1, 4, 1), (SORT, 3), (ARRIVE, 0, 0, 2), (ARRIVE, 1, 1, 2), (SEND, 0, 0, 3, 2),
+    (SORT, 0), (SORT, 1), (ARRIVE, 0, 0, 0), (ARRIVE, 1, 1, 0), (SEND, 0, 0, 3, 0), (SEND, 0, 0, 1, 0),
+    (SEND, 0, 0, 5, 0), (SEND, 0, 0, 2, 0), (SEND, 1, 1, 0, 0), (SEND, 1, 1, 4, 0), (TABLE,), (ARRIVE, 0, 0, 1),
+    (ARRIVE, 1, 1, 1), (SEND, 0, 0, 3, 1), (SEND, 0, 0, 1, 1), (SEND, 0, 0, 5, 1), (SEND, 1, 1, 0, 1),
+    (SEND, 1, 1, 4, 1), (SORT, 2), (SORT, 3), (ARRIVE, 0, 0, 2), (ARRIVE, 1, 1, 2), (SEND, 0, 0, 3, 2),
     (SEND, 0, 0, 1, 2), (SEND, 0, 0, 5, 2), (SEND, 0, 0, 2, 2), (SEND, 1, 1, 0, 2), (SEND, 1, 1, 4, 2), (SORT, 4),
     (ARRIVE, 0, 0, 3), (ARRIVE, 1, 1, 3), (SEND, 0, 0, 2, 3), (SORT, 5), (ARRIVE, 0, 0, 4), (ARRIVE, 1, 1, 4),
     (SORT, 6), (ARRIVE, 0, 0, 5), (ARRIVE, 1, 1, 5), (SEND, 0, 0, 3, 3), (SEND, 0, 0, 1, 3), (SEND, 0, 0, 5, 3),
@@ -34,62 +34,62 @@
     (SEND, 0, 1, 4, 1), (SEND, 0, 5, 7, 1), (SEND, 1, 0, 3, 1), (SEND, 1, 0, 2, 1), (SEND, 0, 2, 9, 0),
     (SEND, 1, 4, 6, 0), (SEND, 1, 0, 5, 1), (ARRIVE, 0, 3, 2), (ARRIVE, 0, 1, 2), (ARRIVE, 0, 5, 2),
     (ARRIVE, 1, 0, 2), (ARRIVE, 1, 4, 2), (ARRIVE, 0, 2, 3), (SEND, 0, 1, 4, 2), (SEND, 1, 0, 3, 2),
-    (SEND, 1, 0, 2, 2), (BEGIN, 0), (BEGIN, 1), (SEND, 1, 0, 5, 2), (SEND, 0, 0, 1, 6), (SEND, 1, 1, 0, 6),
-    (ARRIVE, 0, 3, 3), (ARRIVE, 0, 1, 3), (ARRIVE, 0, 5, 3), (ARRIVE, 1, 0, 3), (ARRIVE, 1, 4, 3), (ARRIVE, 0, 2, 4),
-    (SEND, 0, 1, 4, 3), (SEND, 1, 0, 3, 3), (SEND, 1, 0, 2, 3), (SEND, 0, 5, 7, 3), (ARRIVE, 0, 4, 0),
-    (ARRIVE, 1, 3, 0), (ARRIVE, 1, 5, 0), (ARRIVE, 1, 2, 0), (ARRIVE, 0, 1, 4), (ARRIVE, 1, 0, 4),
+    (SEND, 1, 0, 2, 2), (SEND, 1, 0, 5, 2), (SEND, 0, 0, 1, 6), (SEND, 1, 1, 0, 6), (ARRIVE, 0, 3, 3),
+    (ARRIVE, 0, 1, 3), (ARRIVE, 0, 5, 3), (ARRIVE, 1, 0, 3), (ARRIVE, 1, 4, 3), (ARRIVE, 0, 2, 4),
+    (SEND, 0, 1, 4, 3), (SEND, 1, 0, 3, 3), (SEND, 1, 0, 2, 3), (BEGIN, 0), (BEGIN, 1), (SEND, 0, 5, 7, 3),
+    (ARRIVE, 0, 4, 0), (ARRIVE, 1, 3, 0), (ARRIVE, 1, 5, 0), (ARRIVE, 1, 2, 0), (ARRIVE, 0, 1, 4), (ARRIVE, 1, 0, 4),
     (SEND, 0, 4, 6, 0), (SEND, 1, 2, 9, 0), (SEND, 0, 1, 4, 4), (SEND, 1, 0, 3, 4), (SEND, 1, 0, 2, 4),
     (SEND, 1, 4, 6, 1), (SEND, 0, 0, 3, 4), (SEND, 1, 1, 4, 4), (ARRIVE, 0, 4, 1), (ARRIVE, 0, 7, 1),
     (ARRIVE, 1, 3, 1), (ARRIVE, 1, 2, 1), (ARRIVE, 0, 1, 5), (ARRIVE, 1, 0, 5), (SEND, 0, 7, 2, 1),
     (SEND, 1, 2, 9, 1), (SEND, 1, 0, 2, 5), (SEND, 0, 4, 6, 1), (SEND, 0, 7, 8, 1), (SEND, 1, 0, 5, 3),
     (SEND, 0, 0, 2, 5), (SEND, 0, 1, 4, 5), (SEND, 1, 0, 3, 5), (ARRIVE, 0, 9, 0), (ARRIVE, 1, 6, 0),
-    (ARRIVE, 1, 5, 1), (ARRIVE, 0, 4, 2), (ARRIVE, 1, 3, 2), (ARRIVE, 1, 2, 2), (BEGIN, 3), (BEGIN, 4),
-    (SEND, 0, 4, 6, 2), (SEND, 0, 0, 3, 5), (SEND, 1, 1, 4, 5), (ARRIVE, 1, 5, 2), (ARRIVE, 0, 4, 3),
-    (ARRIVE, 1, 3, 3), (ARRIVE, 1, 2, 3), (ARRIVE, 0, 1, 6), (ARRIVE, 1, 0, 6), (SEND, 1, 5, 7, 2),
-    (SEND, 1, 2, 9, 3), (SEND, 1, 0, 2, 6), (BEGIN, 5), (SEND, 1, 4, 6, 2), (SEND, 0, 2, 9, 3), (SEND, 1, 0, 5, 4),
-    (SEND, 0, 0, 3, 6), (SEND, 0, 0, 2, 6), (SEND, 1, 1, 4, 6), (READY, 0), (READY, 1), (ARRIVE, 0, 6, 0),
-    (ARRIVE, 1, 9, 0), (ARRIVE, 0, 7, 3), (ARRIVE, 0, 4, 4), (ARRIVE, 1, 3, 4), (ARRIVE, 1, 2, 4),
-    (SEND, 1, 2, 7, 0), (SEND, 1, 4, 6, 3), (SEND, 0, 0, 5, 4), (SEND, 0, 1, 4, 6), (SEND, 1, 0, 3, 6), (OWN, 0),
-    (PAIRS, 1, (0,)), (ARRIVE, 0, 2, 1), (ARRIVE, 1, 9, 1), (ARRIVE, 1, 6, 1), (ARRIVE, 0, 3, 4), (ARRIVE, 1, 4, 4),
+    (ARRIVE, 1, 5, 1), (ARRIVE, 0, 4, 2), (ARRIVE, 1, 3, 2), (ARRIVE, 1, 2, 2), (SEND, 0, 4, 6, 2),
+    (SEND, 0, 0, 3, 5), (SEND, 1, 1, 4, 5), (ARRIVE, 1, 5, 2), (ARRIVE, 0, 4, 3), (ARRIVE, 1, 3, 3),
+    (ARRIVE, 1, 2, 3), (ARRIVE, 0, 1, 6), (ARRIVE, 1, 0, 6), (SEND, 1, 5, 7, 2), (SEND, 1, 2, 9, 3),
+    (SEND, 1, 0, 2, 6), (BEGIN, 2), (BEGIN, 3), (BEGIN, 4), (SEND, 1, 4, 6, 2), (SEND, 0, 2, 9, 3),
+    (SEND, 1, 0, 5, 4), (SEND, 0, 0, 3, 6), (SEND, 0, 0, 2, 6), (SEND, 1, 1, 4, 6), (READY, 0), (READY, 1),
+    (ARRIVE, 0, 6, 0), (ARRIVE, 1, 9, 0), (ARRIVE, 0, 7, 3), (ARRIVE, 0, 4, 4), (ARRIVE, 1, 3, 4), (ARRIVE, 1, 2, 4),
+    (BEGIN, 5), (SEND, 1, 2, 7, 0), (SEND, 1, 4, 6, 3), (SEND, 0, 0, 5, 4), (SEND, 0, 1, 4, 6), (SEND, 1, 0, 3, 6),
+    (OWN, 0), (ARRIVE, 0, 2, 1), (ARRIVE, 1, 9, 1), (ARRIVE, 1, 6, 1), (ARRIVE, 0, 3, 4), (ARRIVE, 1, 4, 4),
     (ARRIVE, 1, 2, 5), (SEND, 0, 2, 9, 1), (SEND, 0, 3, 10, 0), (SEND, 1, 6, 11, 0), (SEND, 1, 2, 7, 1),
-    (SEND, 0, 4, 6, 3), (SEND, 1, 2, 9, 4), (SEND, 0, 0, 5, 5), (ARRIVE, 0, 6, 1), (ARRIVE, 0, 8, 1),
-    (ARRIVE, 1, 5, 3), (ARRIVE, 0, 2, 5), (ARRIVE, 0, 4, 5), (ARRIVE, 1, 3, 5), (BEGIN, 2), (SEND, 0, 6, 11, 0),
-    (SEND, 1, 3, 10, 0), (SEND, 0, 2, 7, 2), (SEND, 1, 4, 6, 4), (SEND, 1, 0, 5, 5), (ARRIVE, 0, 6, 2),
-    (ARRIVE, 1, 7, 2), (ARRIVE, 1, 9, 3), (ARRIVE, 0, 3, 5), (ARRIVE, 1, 4, 5), (ARRIVE, 1, 2, 6),
-    (SEND, 1, 7, 8, 2), (BEGIN, 6), (SEND, 0, 3, 10, 1), (SEND, 1, 6, 11, 1), (SEND, 1, 2, 7, 3), (SEND, 0, 4, 6, 4),
+    (SEND, 0, 4, 6, 3), (SEND, 1, 2, 9, 4), (SEND, 0, 0, 5, 5), (PAIRS, 1, (0,)), (ARRIVE, 0, 6, 1),
+    (ARRIVE, 0, 8, 1), (ARRIVE, 1, 5, 3), (ARRIVE, 0, 2, 5), (ARRIVE, 0, 4, 5), (ARRIVE, 1, 3, 5),
+    (SEND, 0, 6, 11, 0), (SEND, 1, 3, 10, 0), (SEND, 0, 2, 7, 2), (SEND, 1, 4, 6, 4), (SEND, 1, 0, 5, 5),
+    (ARRIVE, 0, 6, 2), (ARRIVE, 1, 7, 2), (ARRIVE, 1, 9, 3), (ARRIVE, 0, 3, 5), (ARRIVE, 1, 4, 5), (ARRIVE, 1, 2, 6),
+    (SEND, 1, 7, 8, 2), (SEND, 0, 3, 10, 1), (SEND, 1, 6, 11, 1), (SEND, 1, 2, 7, 3), (SEND, 0, 4, 6, 4),
     (SEND, 1, 2, 9, 5), (SEND, 0, 0, 5, 6), (ARRIVE, 1, 6, 2), (ARRIVE, 0, 9, 3), (ARRIVE, 1, 5, 4),
     (ARRIVE, 0, 3, 6), (ARRIVE, 0, 2, 6), (ARRIVE, 1, 4, 6), (SEND, 1, 9, 8, 0), (SEND, 0, 6, 11, 1),
     (SEND, 1, 3, 10, 1), (SEND, 1, 4, 6, 5), (SEND, 0, 2, 9, 6), (SEND, 1, 0, 5, 6), (READY, 2), (PAIRS, 2, (0, 1)),
     (ARRIVE, 1, 7, 0), (ARRIVE, 0, 9, 1), (ARRIVE, 1, 6, 3), (ARRIVE, 0, 5, 4), (ARRIVE, 0, 4, 6), (ARRIVE, 1, 3, 6),
-    (SEND, 0, 9, 8, 0), (SEND, 0, 6, 11, 2), (SEND, 1, 3, 10, 2), (SEND, 0, 4, 6, 5), (READY, 3), (READY, 4),
-    (ARRIVE, 0, 10, 0), (ARRIVE, 1, 11, 0), (ARRIVE, 1, 7, 1), (ARRIVE, 0, 6, 3), (ARRIVE, 1, 9, 4),
-    (ARRIVE, 0, 5, 5), (SEND, 1, 7, 8, 1), (SEND, 0, 5, 7, 5), (BEGIN, 9), (SEND, 0, 3, 10, 2), (SEND, 1, 6, 11, 2),
+    (BEGIN, 6), (SEND, 0, 9, 8, 0), (SEND, 0, 6, 11, 2), (SEND, 1, 3, 10, 2), (SEND, 0, 4, 6, 5), (READY, 3),
+    (READY, 4), (ARRIVE, 0, 10, 0), (ARRIVE, 1, 11, 0), (ARRIVE, 1, 7, 1), (ARRIVE, 0, 6, 3), (ARRIVE, 1, 9, 4),
+    (ARRIVE, 0, 5, 5), (SEND, 1, 7, 8, 1), (SEND, 0, 5, 7, 5), (SEND, 0, 3, 10, 2), (SEND, 1, 6, 11, 2),
     (SEND, 0, 2, 7, 4), (SEND, 0, 4, 6, 6), (PAIRS, 4, (0, 1, 2)), (ARRIVE, 0, 11, 0), (ARRIVE, 1, 10, 0),
     (ARRIVE, 0, 7, 2), (ARRIVE, 1, 8, 2), (ARRIVE, 1, 6, 4), (ARRIVE, 1, 5, 5), (SEND, 0, 7, 8, 2),
-    (SEND, 1, 8, 9, 2), (BEGIN, 7), (SEND, 0, 3, 10, 3), (SEND, 1, 6, 11, 3), (SEND, 1, 2, 7, 4), (SEND, 1, 2, 9, 6),
+    (SEND, 1, 8, 9, 2), (SEND, 0, 3, 10, 3), (SEND, 1, 6, 11, 3), (SEND, 1, 2, 7, 4), (SEND, 1, 2, 9, 6),
     (SEND, 1, 4, 6, 6), (ARRIVE, 0, 10, 1), (ARRIVE, 1, 11, 1), (ARRIVE, 1, 7, 3), (ARRIVE, 0, 6, 4),
-    (ARRIVE, 1, 9, 5), (ARRIVE, 0, 5, 6), (SEND, 0, 5, 7, 6), (SEND, 0, 6, 11, 3), (SEND, 1, 3, 10, 3),
+    (ARRIVE, 1, 9, 5), (ARRIVE, 0, 5, 6), (SEND, 0, 5, 7, 6), (BEGIN, 7), (SEND, 0, 6, 11, 3), (SEND, 1, 3, 10, 3),
     (SEND, 1, 2, 7, 5), (PAIRS, 3, (2, 4)), (ARRIVE, 1, 8, 0), (ARRIVE, 0, 11, 1), (ARRIVE, 1, 10, 1),
     (ARRIVE, 1, 6, 5), (ARRIVE, 0, 9, 6), (ARRIVE, 1, 5, 6), (SEND, 1, 5, 7, 6), (SEND, 0, 9, 8, 3),
     (SEND, 0, 3, 10, 4), (SEND, 1, 6, 11, 4), (READY, 5), (ARRIVE, 0, 8, 0), (ARRIVE, 1, 8, 1), (ARRIVE, 0, 11, 2),
-    (ARRIVE, 1, 10, 2), (ARRIVE, 0, 7, 5), (ARRIVE, 0, 6, 5), (SEND, 0, 8, 7, 0), (SEND, 0, 7, 8, 5), (BEGIN, 10),
-    (BEGIN, 11), (SEND, 1, 9, 8, 3), (SEND, 0, 6, 11, 4), (SEND, 1, 3, 10, 4), (PAIRS, 5, (1, 3, 4)),
-    (ARRIVE, 0, 10, 2), (ARRIVE, 0, 8, 2), (ARRIVE, 1, 9, 2), (ARRIVE, 1, 11, 2), (ARRIVE, 0, 7, 4),
-    (ARRIVE, 0, 6, 6), (SEND, 0, 8, 9, 2), (SEND, 0, 7, 8, 4), (BEGIN, 8), (SEND, 1, 9, 8, 4), (SEND, 0, 3, 10, 5),
-    (SEND, 1, 6, 11, 5), (ARRIVE, 0, 10, 3), (ARRIVE, 1, 11, 3), (ARRIVE, 1, 7, 4), (ARRIVE, 0, 7, 6),
-    (ARRIVE, 1, 9, 6), (ARRIVE, 1, 6, 6), (SEND, 0, 7, 8, 6), (SEND, 0, 6, 11, 5), (SEND, 1, 3, 10, 5),
-    (SEND, 1, 9, 8, 6), (READY, 6), (ARRIVE, 0, 11, 3), (ARRIVE, 1, 10, 3), (ARRIVE, 1, 7, 5), (ARRIVE, 1, 7, 6),
-    (SEND, 1, 7, 8, 5), (SEND, 0, 3, 10, 6), (SEND, 1, 6, 11, 6), (PAIRS, 6, (0, 2, 5)), (FOLD, (5,)),
-    (ARRIVE, 0, 7, 0), (ARRIVE, 0, 8, 5), (SEND, 0, 8, 9, 5), (ARRIVE, 0, 8, 3), (ARRIVE, 0, 10, 4),
+    (ARRIVE, 1, 10, 2), (ARRIVE, 0, 7, 5), (ARRIVE, 0, 6, 5), (SEND, 0, 8, 7, 0), (SEND, 0, 7, 8, 5),
+    (SEND, 1, 9, 8, 3), (SEND, 0, 6, 11, 4), (SEND, 1, 3, 10, 4), (PAIRS, 5, (1, 3, 4)), (ARRIVE, 0, 10, 2),
+    (ARRIVE, 0, 8, 2), (ARRIVE, 1, 9, 2), (ARRIVE, 1, 11, 2), (ARRIVE, 0, 7, 4), (ARRIVE, 0, 6, 6),
+    (SEND, 0, 8, 9, 2), (SEND, 0, 7, 8, 4), (SEND, 1, 9, 8, 4), (SEND, 0, 3, 10, 5), (SEND, 1, 6, 11, 5),
+    (ARRIVE, 0, 10, 3), (ARRIVE, 1, 11, 3), (ARRIVE, 1, 7, 4), (ARRIVE, 0, 7, 6), (ARRIVE, 1, 9, 6),
+    (ARRIVE, 1, 6, 6), (SEND, 0, 7, 8, 6), (BEGIN, 8), (BEGIN, 10), (BEGIN, 11), (SEND, 0, 6, 11, 5),
+    (SEND, 1, 3, 10, 5), (SEND, 1, 9, 8, 6), (READY, 6), (ARRIVE, 0, 11, 3), (ARRIVE, 1, 10, 3), (ARRIVE, 1, 7, 5),
+    (ARRIVE, 1, 7, 6), (SEND, 1, 7, 8, 5), (SEND, 0, 3, 10, 6), (SEND, 1, 6, 11, 6), (PAIRS, 6, (0, 2, 5)),
+    (FOLD, (5,)), (ARRIVE, 0, 7, 0), (ARRIVE, 0, 8, 5), (SEND, 0, 8, 9, 5), (ARRIVE, 0, 8, 3), (ARRIVE, 0, 10, 4),
     (ARRIVE, 1, 11, 4), (SEND, 0, 6, 11, 6), (SEND, 1, 3, 10, 6), (READY, 7), (ARRIVE, 0, 9, 2), (ARRIVE, 0, 8, 4),
     (SEND, 0, 8, 9, 4), (ARRIVE, 1, 8, 3), (ARRIVE, 0, 11, 4), (ARRIVE, 1, 10, 4), (PAIRS, 7, (1, 3, 4)),
-    (ARRIVE, 0, 8, 6), (ARRIVE, 1, 8, 4), (ARRIVE, 0, 10, 5), (ARRIVE, 1, 11, 5), (PAIRS, 7, (6,)),
-    (ARRIVE, 1, 8, 5), (ARRIVE, 0, 11, 5), (ARRIVE, 1, 10, 5), (ARRIVE, 1, 8, 6), (SHARED, 7, (0,), 2),
-    (ARRIVE, 0, 9, 5), (SHARED, 6, (3,), 0), (READY, 8), (ARRIVE, 0, 10, 6), (ARRIVE, 1, 11, 6), (PAIRS, 8, (3,)),
-    (ARRIVE, 0, 9, 4), (SHARED, 8, (1,), 1), (ARRIVE, 0, 11, 6), (ARRIVE, 1, 10, 6), (READY, 9),
+    (ARRIVE, 0, 8, 6), (BEGIN, 9), (ARRIVE, 1, 8, 4), (ARRIVE, 0, 10, 5), (ARRIVE, 1, 11, 5), (ARRIVE, 1, 8, 5),
+    (PAIRS, 7, (6,)), (ARRIVE, 0, 11, 5), (ARRIVE, 1, 10, 5), (ARRIVE, 1, 8, 6), (ARRIVE, 0, 9, 5),
+    (SHARED, 7, (0,), 2), (READY, 8), (ARRIVE, 0, 10, 6), (ARRIVE, 1, 11, 6), (PAIRS, 8, (3,)), (ARRIVE, 0, 9, 4),
+    (SHARED, 8, (1,), 1), (ARRIVE, 0, 11, 6), (ARRIVE, 1, 10, 6), (SHARED, 6, (3,), 0), (READY, 9),
     (PAIRS, 9, (1, 3, 6)), (FOLD, (1, 3, 6)), (READY, 10), (READY, 11), (PAIRS, 11, (2, 8, 9)), (FOLD, (8,)),
-    (PAIRS, 10, (2, 4, 9)), (FOLD, (2, 4, 9)), (SHARED, 11, (10,), 1), (SHARED, 11, (7,), 0), (FOLD, (11,)),
-    (SHARED, 10, (7,), 0), (FOLD, (7,)), (SHARED, 10, (0,), 0), (FOLD, (0, 10)),
+    (SHARED, 11, (10, 7), 1), (FOLD, (11,)), (PAIRS, 10, (2, 4, 9)), (FOLD, (2, 4, 9)), (SHARED, 10, (7, 0), 0),
+    (FOLD, (0, 7, 10)),
 )
 
 ROWS = 448
@@ -397,8 +397,9 @@
             sent_to(d)
         elif ROOTS[0] != ROOTS[1]:
             on_core(1 - ROOTS.index(d), [functools.partial(sent_to, d)])
-    for d in range(SLOTS):
-        replies(d, "wait_recv")
+    for what in ("wait_send", "wait_recv"):
+        for d in range(SLOTS):
+            replies(d, what)
     incoming[root] = outgoing[root]
     final = []
     for n in (0, 1):
@@ -419,8 +420,6 @@
         jnp.where(sub == 1, middle.astype(jnp.float32), jnp.where(sub == 2, low.astype(jnp.float32), 0.0)),
     ).astype(jnp.bfloat16)
     out[...] = jnp.sum(jnp.dot(parts, table[...], preferred_element_type=jnp.float32), axis=0, keepdims=True)
-    for d in range(SLOTS):
-        replies(d, "wait_send")
 
 
 def local(embeddings, scales, cluster_id, doc_rank):

time: 74.6 us -> 75.1 us (level)
  no operation moved by 1% of the time
where the time goes in v3:
time: 75.1 us; the launch traced here: 74.9 us
  Pallas kernels  73.7 us (98%)
  local copies, waits for them, and re-layouts  1.26 us (2%)
    pallas_call x1, Pallas kernels, local(): pl.pallas_call(kernel, out_shape=jax.ShapeDtypeStruct((1, ROWS), jnp.floa...  73.7 us

profile of v3, /device:TPU:1, one launch (start us, length us, event | category | flops | bytes accessed | tf_op | source)
XLA Modules:
  0.0 74.9 jit_solution(12724523033187322718)
XLA Ops:
  0.0 73.7 %nearest_in_cluster.1 = f32[1,448]{1,0:T(1,128)} custom-call(bf16[448,1024]{1,0:T(8,128)(2,1)} %emb.1, f32[8,448]{1,0:T(8,128)} %bitcast.5, s32[1,448]{1,0:T(1,128)} %bitcast.6, s32[1,448]{1,0:T(1,128)} %bitcast.7), custom_call_target="tpu_custom_call" | custom-call | flops 30000001024 | bytes 1048576 | tf_op jit(solution)/shard_map/nearest_in_cluster/pallas_call | solution.py:428
  73.7 1.3 %copy.6 = f32[448]{0:T(512)} copy(f32[448]{0:T(512)} %bitcast.4) | data formatting | bytes 3584

commit v4 on v2

--- a/solution.py
+++ b/solution.py
@@ -397,8 +397,9 @@
             sent_to(d)
         elif ROOTS[0] != ROOTS[1]:
             on_core(1 - ROOTS.index(d), [functools.partial(sent_to, d)])
-    for d in range(SLOTS):
-        replies(d, "wait_recv")
+    for what in ("wait_send", "wait_recv"):
+        for d in range(SLOTS):
+            replies(d, what)
     incoming[root] = outgoing[root]
     final = []
     for n in (0, 1):
@@ -419,8 +420,6 @@
         jnp.where(sub == 1, middle.astype(jnp.float32), jnp.where(sub == 2, low.astype(jnp.float32), 0.0)),
     ).astype(jnp.bfloat16)
     out[...] = jnp.sum(jnp.dot(parts, table[...], preferred_element_type=jnp.float32), axis=0, keepdims=True)
-    for d in range(SLOTS):
-        replies(d, "wait_send")
 
 
 def local(embeddings, scales, cluster_id, doc_rank):

time: 74.6 us -> 74.5 us (level)
  no operation moved by 1% of the time
where the time goes in v4:
time: 74.5 us; the launch traced here: 74.4 us
  Pallas kernels  73.1 us (98%)
  local copies, waits for them, and re-layouts  1.26 us (2%)
    pallas_call x1, Pallas kernels, local(): pl.pallas_call(kernel, out_shape=jax.ShapeDtypeStruct((1, ROWS), jnp.floa...  73.1 us

profile of v4, /device:TPU:1, one launch (start us, length us, event | category | flops | bytes accessed | tf_op | source)
XLA Modules:
  0.0 74.4 jit_solution(11222246866182631741)
XLA Ops:
  0.0 73.1 %nearest_in_cluster.1 = f32[1,448]{1,0:T(1,128)} custom-call(bf16[448,1024]{1,0:T(8,128)(2,1)} %emb.1, f32[8,448]{1,0:T(8,128)} %bitcast.5, s32[1,448]{1,0:T(1,128)} %bitcast.6, s32[1,448]{1,0:T(1,128)} %bitcast.7), custom_call_target="tpu_custom_call" | custom-call | flops 30000001024 | bytes 1048576 | tf_op jit(solution)/shard_map/nearest_in_cluster/pallas_call | solution.py:428
  73.1 1.3 %copy.6 = f32[448]{0:T(512)} copy(f32[448]{0:T(512)} %bitcast.4) | data formatting | bytes 3584
